TPU v7x, 32 devices: a whole 2x2x4 slice. The times are simulated.
32 devices in a mesh: region: 8 (over z, core), group: 4 (over y, x).
Axes of the slice: x: 2, y: 2, z: 4, core: 2. Of those that a mesh axis runs over, the one named last changes fastest.
Arguments:
- object_slab: float32 [4096, 2, 2048], P('region', None, 'group'), may hold values from -6 to 6
- probe: float32 [4, 2, 256, 256], replicated, may hold values from -6 to 6
- diffraction: float32 [128, 256, 256], P(('region', 'group')), may hold values from 0.25 to 16
- positions: int32 [128, 2], P(('region', 'group')), may hold values from 0 to 3840, as said below
- slot_counts: int32 [4, 8], P('group', 'region'), may hold values from 1 to 4, 20 in all within a row
Outputs:
- new_object: float32 [4096, 2, 2048], P('region', None, 'group')
- new_probe: float32 [4, 2, 256, 256], replicated
Inputs may be any that keep to these rules, and one draw needn't show every extreme that they name: `positions`: A slot of region index r has its row in r * 512 to min(r * 512 + 511, 3840); columns lie in 0 to 256; rows 0 and 3840 and columns 0 and 256 are each taken by some slot.
All inputs are finite; a program needn't handle non-finite values. No bound on the sum of `slot_counts` on one device may be relied on, other than what follows from the above.
Results may differ from a plain program's by a relative error of at most 0.0003.
Values sent between devices are 32-bit elements; how exact they have to be, the bound alone decides.
No kernel may reach another device: no remote copies, remote signals or barrier semaphores. Data moves between devices by JAX's collectives and lax.ppermute only.
A program may use at most 128 MiB of HBM per device.

v0:
```python
import functools
import math

import jax
import jax.numpy as jnp
import numpy as np
from jax import lax
from jax.experimental import pallas as pl
from jax.experimental.pallas import tpu as pltpu
from jax.sharding import PartitionSpec as P

LANES = 128
SUBLANES = 8
ROWS = 32
STREAM = 2
EPSILON = 1e-06


def shifted(block, axis, distance):
    devices = range(lax.axis_size(axis))
    route = [(i - distance, i) for i in devices if i - distance in devices]
    return lax.ppermute(block, axis, route)


def packed(block):
    rows, parts, columns = block.shape
    cut = block.reshape(rows, parts, columns // LANES, LANES).transpose(0, 2, 1, 3)
    return cut.reshape(rows * parts * columns // LANES, LANES)


def unpacked(block, shape):
    rows, parts, columns = shape
    cut = block.reshape(rows, columns // LANES, parts, LANES).transpose(0, 2, 1, 3)
    return cut.reshape(rows, parts, columns)


def tables(side):
    half = side // 2
    n, q = np.arange(half)[:, None], np.arange(half)[None, :]
    made = []
    for odd in range(2):
        angle = 2.0 * math.pi * ((n * (2 * q + odd)) % side) / side
        made += [np.cos(angle) / math.sqrt(side), -np.sin(angle) / math.sqrt(side)]
    return np.stack(made).astype(np.float32)


def fill_table(factor_ref, table_ref):
    half = factor_ref.shape[1]
    left, right = pl.ds(0, half), pl.ds(half, half)
    for odd in range(2):
        for turned in range(2):
            real, imag = factor_ref[2 * odd], factor_ref[2 * odd + 1]
            if turned:
                real, imag = real.T, -imag.T
            for term, (re, im, minus) in enumerate(zip(split(real), split(imag), split(-imag))):
                entry = 2 * turned + odd
                table_ref[term, entry, left, left] = re
                table_ref[term, entry, left, right] = im
                table_ref[term, entry, right, left] = minus
                table_ref[term, entry, right, right] = re


def parity_order(side):
    half = side // 2
    first = lax.broadcasted_iota(jnp.int32, (side, side), 0)
    second = lax.broadcasted_iota(jnp.int32, (side, side), 1)

    def moves(source, place):
        odd = (place >= half).astype(jnp.int32)
        hit = source == 2 * (place - odd * half) + odd
        return hit.astype(jnp.float32).astype(jnp.bfloat16)

    return moves(first, second), moves(second, first)


def split(x):
    high = x.astype(jnp.bfloat16)
    low = (x - high.astype(jnp.float32)).astype(jnp.bfloat16)
    return high, low


def dot(a, b):
    return jnp.dot(a, b, preferred_element_type=jnp.float32)


def transform(terms, rows, table_ref, table, out):
    side = out.shape[2]
    for half in range(2):
        high = terms[half, rows, pl.ds(0, side)]
        low = terms[half, rows, pl.ds(side, side)]
        t_high, t_low = table_ref[0, table + half], table_ref[1, table + half]
        out[half, rows, :] = dot(
            jnp.concatenate([high, low, high], axis=1),
            jnp.concatenate([t_high, t_high, t_low], axis=0),
        )


def transform_rows(terms, rows, table_ref, table, out):
    side = out.shape[2]
    for half in range(2):
        high = terms[half, rows, pl.ds(0, side)]
        low = terms[half, rows, pl.ds(side, side)]
        t_high, t_low = table_ref[0, table + half], table_ref[1, table + half]
        out[half, rows, :] = dot(
            jnp.concatenate([t_high, t_high, t_low], axis=1),
            jnp.concatenate([high, low, high], axis=0),
        )


def keep(terms, half, start, value):
    rows = pl.ds(start, value.shape[0])
    side = value.shape[1]
    high, low = split(value)
    terms[half, rows, pl.ds(0, side)] = high
    terms[half, rows, pl.ds(side, side)] = low


def beside(real, imag):
    return jnp.concatenate([real, imag], axis=1)


def all_slots(
    local,
    tile_rows,
    place_ref,
    count_ref,
    probe_ref,
    table_ref,
    extended,
    gradient,
    sums,
    power,
    measured,
    window,
    terms,
    result,
    back,
):
    modes, _, side, _ = probe_ref.shape
    half = side // 2
    per_row = SUBLANES
    lane = lax.broadcasted_iota(jnp.int32, (side, LANES), 1)
    blocks = side // LANES
    left, right = pl.ds(0, half), pl.ds(half, half)
    pieces = [pl.ds(start, ROWS) for start in range(0, side, ROWS)]
    streams = [range(start, min(start + STREAM, modes)) for start in range(0, modes, STREAM)]

    def rows_of(stream):
        return pl.ds(stream[0] * side, len(stream) * side)

    def slot(index):
        row = place_ref[index, 0]
        column = place_ref[index, 1]
        first = column // LANES
        shift = column - first * LANES
        back_shift = lax.rem(LANES - shift, LANES)
        last = per_row // 2 - 1

        def strided(block, part):
            at = row * per_row + jnp.minimum(first + block, last) * 2 + part
            return pl.ds(at, side, stride=per_row)

        for part in range(2):
            rolled = [
                pltpu.roll(extended[strided(block, part), :], back_shift, 1) for block in range(blocks + 1)
            ]
            for block in range(blocks):
                window[part, :, pl.ds(block * LANES, LANES)] = jnp.where(
                    lane < LANES - shift, rolled[block], rolled[block + 1]
                )
        for stream in streams:
            for mode in stream:
                for rows in pieces:
                    w = [window[part, rows, side_] for part in range(2) for side_ in (left, right)]
                    p = [probe_ref[mode, part, rows, side_] for part in range(2) for side_ in (left, right)]
                    real = [p[k] * w[k] - p[2 + k] * w[2 + k] for k in range(2)]
                    imag = [p[k] * w[2 + k] + p[2 + k] * w[k] for k in range(2)]
                    start = mode * side + rows.start
                    keep(terms, 0, start, beside(real[0] + real[1], imag[0] + imag[1]))
                    keep(terms, 1, start, beside(real[0] - real[1], imag[0] - imag[1]))
            transform(terms, rows_of(stream), table_ref, 0, result)
        halves = [pl.ds(start, ROWS) for start in range(0, half, ROWS)]
        for mode in range(modes):
            base = mode * side
            for rows in halves:
                for part, side_ in enumerate((left, right)):
                    top, bottom = pl.ds(base + rows.start, ROWS), pl.ds(base + half + rows.start, ROWS)
                    above = beside(result[0, top, side_], result[1, top, side_])
                    below = beside(result[0, bottom, side_], result[1, bottom, side_])
                    start = base + part * half + rows.start
                    keep(terms, 0, start, above + below)
                    keep(terms, 1, start, above - below)
            transform_rows(terms, pl.ds(base, side), table_ref, 2, result)
        for odd in range(2):
            for rows in halves:
                far = [
                    [result[odd, pl.ds(mode * side + part * half + rows.start, ROWS), :] for part in range(2)]
                    for mode in range(modes)
                ]
                intensity = jnp.zeros((ROWS, side), jnp.float32)
                for real, imag in far:
                    intensity = intensity + real * real + imag * imag
                amount = measured[index, pl.ds(odd * half + rows.start, ROWS), :]
                ratio = amount * lax.rsqrt(amount * jnp.maximum(intensity, 1.0))
                for mode in range(modes):
                    for part in range(2):
                        keep(terms, odd, mode * side + part * half + rows.start, far[mode][part] * ratio)
        for mode in range(modes):
            transform_rows(terms, pl.ds(mode * side, side), table_ref, 0, result)
        for stream in streams:
            for mode in stream:
                base = mode * side
                for rows in halves:
                    real, imag = pl.ds(base + rows.start, ROWS), pl.ds(base + half + rows.start, ROWS)
                    for odd, side_ in enumerate((left, right)):
                        a = beside(result[0, real, side_], result[0, imag, side_])
                        b = beside(result[1, real, side_], result[1, imag, side_])
                        keep(terms, odd, base + rows.start, a + b)
                        keep(terms, odd, base + half + rows.start, a - b)
            transform(terms, rows_of(stream), table_ref, 2, result)
        for number, stream in enumerate(streams):
            for rows in pieces:
                chunk = pl.ds(rows.start // SUBLANES, ROWS // SUBLANES)
                by_chunk = (ROWS // SUBLANES, SUBLANES, half)
                for lower, side_ in enumerate((left, right)):
                    w_r, w_i = window[0, rows, side_], window[1, rows, side_]
                    if number:
                        g_r, g_i = back[0, rows, side_], back[1, rows, side_]
                    else:
                        strength = power[rows, side_]
                        g_r, g_i = strength * w_r, strength * w_i
                    for mode in stream:
                        at = pl.ds(mode * side + rows.start, ROWS)
                        if lower:
                            c_r = result[0, at, left] - result[1, at, left]
                            c_i = result[0, at, right] - result[1, at, right]
                        else:
                            c_r = result[0, at, left] + result[1, at, left]
                            c_i = result[0, at, right] + result[1, at, right]
                        p_r, p_i = probe_ref[mode, 0, rows, side_], probe_ref[mode, 1, rows, side_]
                        g_r = g_r - (p_r * c_r + p_i * c_i)
                        g_i = g_i - (p_r * c_i - p_i * c_r)
                        sums[chunk, 2 * mode, :, side_] += (w_r * c_r + w_i * c_i).reshape(by_chunk)
                        sums[chunk, 2 * mode + 1, :, side_] += (w_r * c_i - w_i * c_r).reshape(by_chunk)
                    back[0, rows, side_] = g_r
                    back[1, rows, side_] = g_i
                    if not number:
                        sums[chunk, 2 * modes, :, side_] += (w_r * w_r + w_i * w_i).reshape(by_chunk)

        for part in range(2):
            rolled = [
                pltpu.roll(back[part, :, pl.ds(block * LANES, LANES)], shift, 1) for block in range(blocks)
            ]
            zero = jnp.zeros((side, LANES), jnp.float32)
            for block in range(blocks + 1):
                here = rolled[block] if block < blocks else zero
                before = rolled[block - 1] if block else zero
                at = strided(block, part)
                gradient[at, :] = gradient[at, :] + jnp.where(lane >= shift, here, before)

    def visit(index, carry):
        inside = place_ref[index, 0] + side <= tile_rows
        pl.when(inside if local else jnp.logical_not(inside))(lambda: slot(index))
        return carry

    lax.fori_loop(0, count_ref[0, 0], visit, 0)


def first_kernel(
    place_ref,
    count_ref,
    tile_hbm,
    probe_ref,
    diffraction_ref,
    factor_ref,
    tile_out,
    gradient,
    sums,
    measured,
    power,
    probe_out,
    table_out,
    scale_out,
    window,
    terms,
    result,
    back,
    semaphore,
):
    modes, _, side, _ = probe_ref.shape
    copy = pltpu.make_async_copy(tile_hbm, tile_out, semaphore)
    copy.start()
    gradient[...] = jnp.zeros_like(gradient)
    sums[...] = jnp.zeros_like(sums)
    total = jnp.zeros((side, side), jnp.float32)
    for mode in range(modes):
        total = total + probe_ref[mode, 0] * probe_ref[mode, 0] + probe_ref[mode, 1] * probe_ref[mode, 1]
    power[...] = total
    scale_out[...] = jnp.full(scale_out.shape, 1.0 / jnp.max(total))
    probe_out[...] = probe_ref[...]
    fill_table(factor_ref, table_out)
    by_lanes, by_rows = parity_order(side)

    def order(index, carry):
        high, low = split(diffraction_ref[index])
        seen = dot(jnp.concatenate([by_rows] * 2, axis=1), jnp.concatenate([high, low], axis=0))
        high, low = split(seen)
        seen = dot(jnp.concatenate([high, low], axis=1), jnp.concatenate([by_lanes] * 2, axis=0))
        measured[index] = seen
        return carry

    lax.fori_loop(0, count_ref[0, 0], order, 0)
    copy.wait()
    all_slots(
        True, tile_out.shape[0] // SUBLANES, place_ref, count_ref, probe_ref, table_out, tile_out,
        gradient, sums, power, measured, window, terms, result, back,
    )


def second_kernel(
    place_ref,
    count_ref,
    here_ref,
    halo_ref,
    tile_ref,
    gradient_ref,
    sums_ref,
    measured,
    power,
    probe_ref,
    table_ref,
    gradient,
    spill_out,
    mine_out,
    near_out,
    far_out,
    old_out,
    extended,
    sums,
    window,
    terms,
    result,
    back,
):
    modes = probe_ref.shape[0]
    tile_rows, halo_rows, chunks = tile_ref.shape[0], halo_ref.shape[0], sums.shape[0]
    extended[pl.ds(0, tile_rows), :] = tile_ref[...]
    extended[pl.ds(tile_rows, halo_rows), :] = halo_ref[...]
    gradient[pl.ds(0, tile_rows), :] = gradient_ref[...]
    gradient[pl.ds(tile_rows, halo_rows), :] = jnp.zeros((halo_rows, LANES), jnp.float32)
    sums[...] = sums_ref[...]
    all_slots(
        False, tile_rows // SUBLANES, place_ref, count_ref, probe_ref, table_ref, extended,
        gradient, sums, power, measured, window, terms, result, back,
    )
    spill_out[...] = gradient[pl.ds(tile_rows, halo_rows), :]
    core, group, layer = here_ref[0, 0], here_ref[0, 1], here_ref[0, 2]
    groups, layers = mine_out.shape[0], mine_out.shape[1]
    for hop in range(groups):
        for step in range(layers):
            at = (group ^ hop) * layers + lax.rem(layer + step, layers)
            mine_out[hop, step] = sums[core * (chunks // 2) + at]
            if hop < groups - 1:
                near_out[hop, step] = sums[(1 - core) * (chunks // 2) + at]
            else:
                far_out[step] = sums[(1 - core) * (chunks // 2) + at]
    start = pl.multiple_of(((core * groups + group) * layers + layer) * SUBLANES, SUBLANES)
    for mode in range(modes):
        for part in range(2):
            old_out[2 * mode + part] = probe_ref[mode, part, pl.ds(start, SUBLANES), :]


def gradient_step(place, count, here, tile, halo, probe, diffraction, groups, layers):
    modes, parts, side, _ = probe.shape
    planes = parts * modes + 1
    chunks = side // SUBLANES
    f32 = jnp.float32
    smem = pl.BlockSpec(memory_space=pltpu.SMEM)
    vmem = pl.BlockSpec(memory_space=pltpu.VMEM)
    chunk = (planes, SUBLANES, side)
    products = 3 * 16 * modes * diffraction.shape[0] * side**3 // 2
    work = [
        pltpu.VMEM((2, side, side), f32),
        pltpu.VMEM((2, modes * side, 2 * side), jnp.bfloat16),
        pltpu.VMEM((2, modes * side, side), f32),
        pltpu.VMEM((2, side, side), f32),
    ]
    shape = jax.ShapeDtypeStruct
    cost = pl.CostEstimate(flops=2 * products, bytes_accessed=16 << 20, transcendentals=0)
    *begun, scale = pl.pallas_call(
        first_kernel,
        out_shape=(
            shape(tile.shape, f32),
            shape(tile.shape, f32),
            shape((chunks, *chunk), f32),
            shape(diffraction.shape, f32),
            shape((side, side), f32),
            shape(probe.shape, f32),
            shape((2, 4, side, side), jnp.bfloat16),
            shape((1, LANES), f32),
        ),
        in_specs=[smem, smem, pl.BlockSpec(memory_space=pl.ANY), vmem, vmem, vmem],
        out_specs=(vmem,) * 8,
        scratch_shapes=work + [pltpu.SemaphoreType.DMA],
        compiler_params=pltpu.CompilerParams(vmem_limit_bytes=28 * 1024 * 1024),
        cost_estimate=cost,
        name="slots_inside",
    )(place, count, tile, probe, diffraction, jnp.asarray(tables(side)))
    gradient, *rest = pl.pallas_call(
        second_kernel,
        out_shape=(
            shape((tile.shape[0] + halo.shape[0], LANES), f32),
            shape(halo.shape, f32),
            shape((groups, layers, *chunk), f32),
            shape((groups - 1, layers, *chunk), f32),
            shape((layers, *chunk), f32),
            shape((planes - 1, SUBLANES, side), f32),
        ),
        in_specs=[smem, smem, smem] + [vmem] * 8,
        out_specs=(vmem,) * 6,
        scratch_shapes=[
            pltpu.VMEM((tile.shape[0] + halo.shape[0], LANES), f32),
            pltpu.VMEM((chunks, *chunk), f32),
        ]
        + work,
        compiler_params=pltpu.CompilerParams(vmem_limit_bytes=30 * 1024 * 1024),
        cost_estimate=cost,
        name="slots_across",
    )(place, count, here, halo, *begun)
    new_tile, top = written(begun[0], gradient, scale, halo.shape[0])
    return new_tile, top, scale, *rest


def write_kernel(tile_ref, gradient_ref, scale_ref, out_ref, top_ref, rows, semaphores):
    scale = scale_ref[...]
    step = out_ref.shape[0] // 4
    copies = []
    for part in range(4):
        at = pl.ds(part * step, step)
        rows[at, :] = tile_ref[at, :] - gradient_ref[at, :] * scale
        copies.append(pltpu.make_async_copy(rows.at[at], out_ref.at[at], semaphores.at[part]))
        copies[-1].start()
    top_ref[...] = rows[pl.ds(0, top_ref.shape[0]), :]
    for copy in copies:
        copy.wait()


def written(tile, gradient, scale, top_rows):
    vmem, anywhere = pl.BlockSpec(memory_space=pltpu.VMEM), pl.BlockSpec(memory_space=pl.ANY)
    return pl.pallas_call(
        write_kernel,
        out_shape=(
            jax.ShapeDtypeStruct(tile.shape, jnp.float32),
            jax.ShapeDtypeStruct((top_rows, LANES), jnp.float32),
        ),
        in_specs=[vmem, vmem, vmem],
        out_specs=(anywhere, vmem),
        scratch_shapes=[pltpu.VMEM(tile.shape, jnp.float32), pltpu.SemaphoreType.DMA((4,))],
        compiler_params=pltpu.CompilerParams(vmem_limit_bytes=10 * 1024 * 1024),
        cost_estimate=pl.CostEstimate(flops=0, bytes_accessed=4 << 20, transcendentals=0),
        name="written",
    )(tile, gradient, scale)


def first_rows(tile, rows):
    def kernel(tile_ref, out_ref, semaphore):
        copy = pltpu.make_async_copy(tile_ref.at[pl.ds(0, rows)], out_ref, semaphore)
        copy.start()
        copy.wait()

    return pl.pallas_call(
        kernel,
        out_shape=jax.ShapeDtypeStruct((rows, LANES), jnp.float32),
        in_specs=[pl.BlockSpec(memory_space=pl.ANY)],
        out_specs=pl.BlockSpec(memory_space=pltpu.VMEM),
        scratch_shapes=[pltpu.SemaphoreType.DMA],
        compiler_params=pltpu.CompilerParams(vmem_limit_bytes=4 * 1024 * 1024),
        cost_estimate=pl.CostEstimate(flops=0, bytes_accessed=16 << 20, transcendentals=0),
        name="first_rows",
    )(tile)


def divide_kernel(old_ref, *refs):
    *parts, out_ref = refs
    total = parts[0][...]
    for part in parts[1:]:
        total = total + part[...]
    out_ref[...] = (EPSILON * old_ref[...] + total[:-1]) / (total[-1:] + EPSILON)


def divided(old, parts):
    return pl.pallas_call(
        divide_kernel,
        out_shape=jax.ShapeDtypeStruct(old.shape, jnp.float32),
        compiler_params=pltpu.CompilerParams(vmem_limit_bytes=4 * 1024 * 1024),
        name="divided",
    )(old, *parts)


def place_kernel(layers, pieces, here_ref, *refs):
    sources, out, semaphores = refs[: len(pieces)], refs[-2], refs[-1]
    core, group, layer = here_ref[0, 0], here_ref[0, 1], here_ref[0, 2]
    copies = []
    for source, (flip, hop, start) in zip(sources, pieces):
        for j in range(source.shape[0]):
            from_layer = lax.rem(layer + layers - (start + j), layers)
            at = (core ^ flip) * (out.shape[1] // 2) + (group ^ hop) * layers + from_layer
            copies.append(pltpu.make_async_copy(source.at[j], out.at[:, at], semaphores.at[len(copies)]))
    for copy in copies:
        copy.start()
    for copy in copies:
        copy.wait()


def put_in_place(here, layers, pieces, arrays, planes, side, held=None):
    vmem, anywhere = pl.BlockSpec(memory_space=pltpu.VMEM), pl.BlockSpec(memory_space=pl.ANY)
    rest = [] if held is None else [held]
    return pl.pallas_call(
        functools.partial(place_kernel, layers, pieces),
        out_shape=jax.ShapeDtypeStruct((planes, side // SUBLANES, SUBLANES, side), jnp.float32),
        in_specs=[pl.BlockSpec(memory_space=pltpu.SMEM)] + [vmem] * len(arrays) + [anywhere] * len(rest),
        out_specs=anywhere,
        scratch_shapes=[pltpu.SemaphoreType.DMA((sum(array.shape[0] for array in arrays),))],
        input_output_aliases={} if held is None else {1 + len(arrays): 0},
        compiler_params=pltpu.CompilerParams(vmem_limit_bytes=8 * 1024 * 1024),
        cost_estimate=pl.CostEstimate(flops=0, bytes_accessed=4 << 20, transcendentals=0),
        name="put_in_place",
    )(here, *arrays, *rest)


def top_kernel(held_ref, top_ref, arrived_ref, scale_ref, out_ref, rows, semaphore):
    rows[...] = top_ref[...] - arrived_ref[...] * scale_ref[...]
    copy = pltpu.make_async_copy(rows, out_ref.at[pl.ds(0, rows.shape[0])], semaphore)
    copy.start()
    copy.wait()


def with_top(tile, top, arrived, scale):
    vmem, anywhere = pl.BlockSpec(memory_space=pltpu.VMEM), pl.BlockSpec(memory_space=pl.ANY)
    return pl.pallas_call(
        top_kernel,
        out_shape=jax.ShapeDtypeStruct(tile.shape, jnp.float32),
        in_specs=[anywhere, vmem, vmem, vmem],
        out_specs=anywhere,
        scratch_shapes=[pltpu.VMEM(top.shape, jnp.float32), pltpu.SemaphoreType.DMA],
        input_output_aliases={0: 0},
        compiler_params=pltpu.CompilerParams(vmem_limit_bytes=8 * 1024 * 1024),
        cost_estimate=pl.CostEstimate(flops=0, bytes_accessed=2 << 20, transcendentals=0),
        name="with_top",
    )(tile, top, arrived, scale)


def across(block, hop):
    return lax.ppermute(block, "group", [(i, i ^ hop) for i in range(lax.axis_size("group"))])


def from_partner(block):
    return lax.ppermute(block, "region", [(i, i ^ 1) for i in range(lax.axis_size("region"))])


def up_layers(block, step):
    regions = lax.axis_size("region")
    return lax.ppermute(block, "region", [(i, (i + 2 * step) % regions) for i in range(regions)])


def probe_by_shards(probe, mine, near, far, old, here, layers, spill, new_tile, top, scale):
    modes, parts, side, _ = probe.shape
    planes = modes * parts
    half = layers // 2
    near, other_far = lax.optimization_barrier((near, from_partner(far)))
    other_near, spill = lax.optimization_barrier((from_partner(near), spill))
    arrived = shifted(spill, "region", 1)
    far_sum = mine[3] + other_far
    by_x, by_y = across(far_sum[:half], 1), across(far_sum[half:], 2)
    near_sum = mine[:3] + other_near
    to_x = near_sum[1].at[half:].add(by_y)
    to_y = near_sum[2].at[:half].add(by_x)
    by_x, by_y, new_tile, top = lax.optimization_barrier((across(to_x, 1), across(to_y, 2), new_tile, top))
    summed = [near_sum[0, step] + by_x[step] + by_y[step] for step in range(layers)]
    *others, arrived = lax.optimization_barrier(
        (*[up_layers(summed[step], step) for step in range(1, layers)], arrived)
    )
    new_tile = with_top(new_tile, top, arrived, scale)
    fresh = divided(old, [summed[0]] + others)
    *others, new_tile = lax.optimization_barrier(
        (*[up_layers(fresh, step) for step in range(1, layers)], new_tile)
    )
    own = jnp.stack([fresh] + others)
    x, y = across(own, 1), across(own, 2)
    far = [across(x[:half], 2), across(y[half:], 1)]
    near = [own, x, y, from_partner(own), from_partner(x), from_partner(y)]
    placed = put_in_place(
        here, layers, tuple((flip, hop, 0) for flip in range(2) for hop in range(3)), near, planes, side
    )
    *far, placed = lax.optimization_barrier((*far, placed))
    far = far + [from_partner(array) for array in far]
    pieces = tuple((flip, 3, start) for flip in range(2) for start in (0, half))
    placed = put_in_place(here, layers, pieces, far, planes, side, placed)
    return placed.reshape(probe.shape), new_tile


def probe_from_whole(probe, mine, near, far):
    side = probe.shape[2]
    own = mine.reshape(-1, *mine.shape[2:])
    rest = jnp.concatenate([near.reshape(-1, *near.shape[2:]), far])
    whole = lax.psum(jnp.concatenate([own, rest]), ("region", "group"))
    whole = whole.transpose(1, 0, 2, 3).reshape(-1, side, side)
    old = probe.reshape(-1, side, side)
    return ((EPSILON * old + whole[:-1]) / (whole[-1:] + EPSILON)).reshape(probe.shape)


def on_device(object_slab, probe, diffraction, positions, slot_counts):
    modes, parts, side, _ = probe.shape
    tile_rows, _, columns = object_slab.shape
    regions, groups = lax.axis_size("region"), lax.axis_size("group")
    region, group = lax.axis_index("region"), lax.axis_index("group")
    per_row = parts * columns // LANES
    assert per_row == SUBLANES
    layers = regions // 2
    sharded = groups == 4 and 2 * groups * layers * SUBLANES == side
    tile = packed(object_slab)
    halo = shifted(first_rows(tile, side * per_row), "region", -1)
    place = positions - jnp.stack([region * tile_rows, jnp.zeros_like(region)])[None, :].astype(jnp.int32)
    if sharded:
        here = jnp.stack([region % 2, group, region // 2]).astype(jnp.int32).reshape(1, 3)
    else:
        here = jnp.zeros((1, 3), jnp.int32)
        groups, layers = 4, side // SUBLANES // 8
    new_tile, top, scale, spill, mine, near, far, old = gradient_step(
        place, slot_counts, here, tile, halo, probe, diffraction, groups, layers
    )
    if sharded:
        new_probe, new_tile = probe_by_shards(
            probe, mine, near, far, old, here, layers, spill, new_tile, top, scale
        )
    else:
        new_tile = with_top(new_tile, top, shifted(spill, "region", 1), scale)
        new_probe = probe_from_whole(probe, mine, near, far)
    return (unpacked(new_tile, object_slab.shape), new_probe)


def solution(mesh):
    placed = (
        P("region", None, "group"),
        P(),
        P(("region", "group"), None, None),
        P(("region", "group"), None),
        P("group", "region"),
    )
    return jax.shard_map(
        on_device,
        mesh=mesh,
        in_specs=placed,
        out_specs=(P("region", None, "group"), P()),
        check_vma=False,
    )
```

profile of v0, /device:TPU:0, one launch (start us, length us, event | category | flops | bytes accessed | tf_op | source)
XLA Modules:
  0.0 90.7 jit_solution(12034863497317383812)
XLA Ops:
  0.6 0.0 copy-start.5
  0.6 0.0 copy-start
  0.6 1.6 %copy-done = f32[512,2,512]{2,1,0:T(2,128)S(1)} copy-done((f32[512,2,512]{2,1,0:T(2,128)S(1)}, f32[512,2,512]{2,1,0:T(2,128)}, u32[]{:S(2)}) %copy-start) | copy-done | bytes 2097176
  2.2 0.1 first_rows.1
  2.3 1.4 %collective-permute-start = (f32[2048,128]{1,0:T(8,128)S(1)}, f32[2048,128]{1,0:T(8,128)}, u32[]{:S(2)}, u32[]{:S(2)}) collective-permute-start(f32[2048,128]{1,0:T(8,128)S(1)} %first_rows.1), channel_id=1, source_target_pairs={{4,0},{8,4},{12,8},{16,12},{20,16},{24,20},{28,24},{5,1},{9,5},{13... | collective-permute-start | bytes 3145736 | tf_op jit(solution)/shard_map/ppermute | solution.py:22
  4.4 0.0 copy-done.5
  4.4 0.1 copy.10
  4.5 0.1 pad_add_fusion
  4.6 0.1 add_bitcast_fusion.here_ref
  4.7 1.6 %copy-done.2 = f32[4,2,256,256]{3,2,1,0:T(8,128)S(1)} copy-done((f32[4,2,256,256]{3,2,1,0:T(8,128)S(1)}, f32[4,2,256,256]{3,2,1,0:T(8,128)}, u32[]{:S(2)}) %copy-start.2) | copy-done | bytes 2097176
  6.3 1.2 %copy-done.3 = f32[4,256,256]{2,1,0:T(8,128)S(1)} copy-done((f32[4,256,256]{2,1,0:T(8,128)S(1)}, f32[4,256,256]{2,1,0:T(8,128)}, u32[]{:S(2)}) %copy-start.3) | copy-done | bytes 1048600
  7.5 13.9 %slots_inside.1 = (f32[4096,128]{1,0:T(8,128)S(1)}, f32[4096,128]{1,0:T(8,128)S(1)}, f32[32,9,8,256]{3,2,1,0:T(8,128)S(1)}, f32[4,256,256]{2,1,0:T(8,128)S(1)}, ...) custom-call(s32[4,2]{1,0:T(4,128)S(1)} %broadcast_subtract_fusion.pl, ...), custom_call_target="tpu_custom_call" | custom-call | flops 12884901888 | bytes 16777216 | tf_op jit(solution)/shard_map/slots_inside/pallas_call | solution.py:390
  21.4 0.0 collective-permute-done.halo_ref
  21.4 12.5 %slots_across.1 = (f32[6144,128]{1,0:T(8,128)S(1)}, f32[2048,128]{1,0:T(8,128)S(1)}, f32[4,4,9,8,256]{4,3,2,1,0:T(8,128)S(1)}, f32[3,4,9,8,256]{4,3,2,1,0:T(8,12...) custom-call(s32[4,2]{1,0:T(4,128)S(1)} %broadcast_subtract_fusion.place_ref, s32[1,1]{1,0:T(1,128)S(6)} %copy.17.count_ref, ...), custom_call_target="tpu_custom_call" | custom-call | flops 12884901888 | bytes 16777216 | tf_op jit(solution)/shard_map/slots_across/pallas_call | solution.py:409
  33.9 0.1 collective-permute-start.1
  34.0 1.6 %collective-permute-done.1 = f32[4,9,8,256]{3,2,1,0:T(8,128)S(1)} collective-permute-done((f32[4,9,8,256]{3,2,1,0:T(8,128)S(1)}, f32[4,9,8,256]{3,2,1,0:T(8,128)S(1)}, u32[]{:S(2)}, u32[]{:S(2)}) %collective-permute-start.1) | collective-permute-done | bytes 294944 | tf_op jit(solution)/shard_map/ppermute | solution.py:558
  35.5 0.1 collective-permute-start.2
  35.7 0.1 collective-permute-start.5
  35.8 0.1 collective-permute-start.3
  35.9 2.1 %collective-permute-done.2 = f32[3,4,9,8,256]{4,3,2,1,0:T(8,128)S(1)} collective-permute-done((f32[3,4,9,8,256]{4,3,2,1,0:T(8,128)S(1)}, f32[3,4,9,8,256]{4,3,2,1,0:T(8,128)S(1)}, u32[]{:S(2)}, u32[]{:S(2)}) %collective-permute-start.2) | collective-permute-done | bytes 884768 | tf_op jit(solution)/shard_map/ppermute | solution.py:558
  38.0 0.1 slice_add_fusion
  38.1 2.3 %collective-permute-start.10 = (f32[2048,128]{1,0:T(8,128)S(1)}, f32[2048,128]{1,0:T(8,128)S(1)}, u32[]{:S(2)}, u32[]{:S(2)}) collective-permute-start(f32[2048,128]{1,0:T(8,128)S(1)} %get-tuple-element.82), channel_id=1, source_target_pairs={{0,4},{4,8},{8,12},{12,16},{16,20},{20,24},{24,28},{1,5},{5,9},{9,... | collective-permute-start | bytes 3145736 | tf_op jit(solution)/shard_map/ppermute | solution.py:22
  40.4 1.5 %collective-permute-done.5 = f32[2,9,8,256]{3,2,1,0:T(8,128)S(1)} collective-permute-done((f32[2,9,8,256]{3,2,1,0:T(8,128)S(1)}, f32[2,9,8,256]{3,2,1,0:T(8,128)S(1)}, u32[]{:S(2)}, u32[]{:S(2)}) %collective-permute-start.5) | collective-permute-done | bytes 147488 | tf_op jit(solution)/shard_map/ppermute | solution.py:554
  41.9 0.1 collective-permute-done.3
  42.0 0.4 collective-permute-start.6
  42.4 1.7 %collective-permute-start.4 = (f32[4,9,8,256]{3,2,1,0:T(8,128)S(1)}, f32[4,9,8,256]{3,2,1,0:T(8,128)S(1)}, u32[]{:S(2)}, u32[]{:S(2)}) collective-permute-start(f32[4,9,8,256]{3,2,1,0:T(8,128)S(1)} %get-tuple-element.101), channel_id=1, source_target_pairs={{0,1},{1,0},{2,3},{3,2},{4,5},{5,4},{6,7},{7,6},{8,9},{9,8},{10,11... | collective-permute-start | bytes 884744 | tf_op jit(solution)/shard_map/ppermute | solution.py:554
  44.1 1.4 %written.1 = (f32[4096,128]{1,0:T(8,128)}, f32[2048,128]{1,0:T(8,128)S(1)}) custom-call(f32[4096,128]{1,0:T(8,128)S(1)} %get-tuple-element.61.tile_ref, f32[6144,128]{1,0:T(8,128)S(1)} %get-tuple-element.76.gradient_ref, f32[1,128]{1,0:T(1,128)S(1)} %get-tuple-element.77.scale_ref), custom_call_target="tpu_custom_call" | custom-call | bytes 4194304 | tf_op jit(solution)/shard_map/written/pallas_call | solution.py:450
  45.5 3.3 %collective-permute-done.6 = f32[4,9,8,256]{3,2,1,0:T(8,128)S(1)} collective-permute-done((f32[4,9,8,256]{3,2,1,0:T(8,128)S(1)}, f32[4,9,8,256]{3,2,1,0:T(8,128)S(1)}, u32[]{:S(2)}, u32[]{:S(2)}) %collective-permute-start.6) | collective-permute-done | bytes 294944 | tf_op jit(solution)/shard_map/ppermute | solution.py:554
  48.8 0.3 collective-permute-done.4
  49.1 0.1 fusion.5
  49.2 4.3 %collective-permute-start.9 = (f32[9,8,256]{2,1,0:T(8,128)S(1)}, f32[9,8,256]{2,1,0:T(8,128)S(1)}, u32[]{:S(2)}, u32[]{:S(2)}) collective-permute-start(f32[9,8,256]{2,1,0:T(8,128)S(1)} %get-tuple-element.96), channel_id=1, source_target_pairs={{0,24},{4,28},{8,0},{12,4},{16,8},{20,12},{24,16},{28,20},{1,25},{... | collective-permute-start | bytes 221192 | tf_op jit(solution)/shard_map/ppermute | solution.py:563
  53.5 5.6 %collective-permute-start.8 = (f32[9,8,256]{2,1,0:T(8,128)S(1)}, f32[9,8,256]{2,1,0:T(8,128)S(1)}, u32[]{:S(2)}, u32[]{:S(2)}) collective-permute-start(f32[9,8,256]{2,1,0:T(8,128)S(1)} %get-tuple-element.97), channel_id=1, source_target_pairs={{0,16},{4,20},{8,24},{12,28},{16,0},{20,4},{24,8},{28,12},{1,17},{... | collective-permute-start | bytes 221192 | tf_op jit(solution)/shard_map/ppermute | solution.py:563
  59.1 0.0 collective-permute-start.7
  59.1 1.4 %collective-permute-done.9.refs_3_ = f32[9,8,256]{2,1,0:T(8,128)S(1)} collective-permute-done((f32[9,8,256]{2,1,0:T(8,128)S(1)}, f32[9,8,256]{2,1,0:T(8,128)S(1)}, u32[]{:S(2)}, u32[]{:S(2)}) %collective-permute-start.9) | collective-permute-done | bytes 73760 | tf_op jit(solution)/shard_map/ppermute | solution.py:563
  60.5 3.3 %collective-permute-done.8.refs_2_ = f32[9,8,256]{2,1,0:T(8,128)S(1)} collective-permute-done((f32[9,8,256]{2,1,0:T(8,128)S(1)}, f32[9,8,256]{2,1,0:T(8,128)S(1)}, u32[]{:S(2)}, u32[]{:S(2)}) %collective-permute-start.8) | collective-permute-done | bytes 73760 | tf_op jit(solution)/shard_map/ppermute | solution.py:563
  63.8 1.5 %collective-permute-done.7.refs_1_ = f32[9,8,256]{2,1,0:T(8,128)S(1)} collective-permute-done((f32[9,8,256]{2,1,0:T(8,128)S(1)}, f32[9,8,256]{2,1,0:T(8,128)S(1)}, u32[]{:S(2)}, u32[]{:S(2)}) %collective-permute-start.7) | collective-permute-done | bytes 73760 | tf_op jit(solution)/shard_map/ppermute | solution.py:563
  65.2 0.0 collective-permute-done.10.arrived_ref
  65.3 0.2 collective-permute-start.13
  65.5 1.3 %collective-permute-start.12 = (f32[8,8,256]{2,1,0:T(8,128)S(1)}, f32[8,8,256]{2,1,0:T(8,128)S(1)}, u32[]{:S(2)}, u32[]{:S(2)}) collective-permute-start(f32[8,8,256]{2,1,0:T(8,128)S(1)} %divided.1), channel_id=1, source_target_pairs={{0,16},{4,20},{8,24},{12,28},{16,0},{20,4},{24,8},{28,12},{1,17},{... | collective-permute-start | bytes 196616 | tf_op jit(solution)/shard_map/ppermute | solution.py:563
  66.7 1.0 %collective-permute-start.11 = (f32[8,8,256]{2,1,0:T(8,128)S(1)}, f32[8,8,256]{2,1,0:T(8,128)S(1)}, u32[]{:S(2)}, u32[]{:S(2)}) collective-permute-start(f32[8,8,256]{2,1,0:T(8,128)S(1)} %divided.1), channel_id=1, source_target_pairs={{0,8},{4,12},{8,16},{12,20},{16,24},{20,28},{24,0},{28,4},{1,9},{5... | collective-permute-start | bytes 196616 | tf_op jit(solution)/shard_map/ppermute | solution.py:563
  67.8 1.1 %with_top.1 = f32[4096,128]{1,0:T(8,128)} custom-call(f32[4096,128]{1,0:T(8,128)} %get-tuple-element.86.held_ref, f32[2048,128]{1,0:T(8,128)S(1)} %get-tuple-element.87.top_ref, f32[2048,128]{1,0:T(8,128)S(1)} %collective-permute-done.10.arrived_ref, f32[1,128]{1,0:T(1,128)S(1)} %get-tuple-element.77.scale_ref), custom_call_target="tpu_custom_call", output_to_operand_aliasing={{}: (0, {})} | custom-call | bytes 2097152 | tf_op jit(solution)/shard_map/with_top/pallas_call | solution.py:540
  68.8 0.9 collective-permute-done.13
  69.7 2.4 %collective-permute-done.12 = f32[8,8,256]{2,1,0:T(8,128)S(1)} collective-permute-done((f32[8,8,256]{2,1,0:T(8,128)S(1)}, f32[8,8,256]{2,1,0:T(8,128)S(1)}, u32[]{:S(2)}, u32[]{:S(2)}) %collective-permute-start.12) | collective-permute-done | bytes 65568 | tf_op jit(solution)/shard_map/ppermute | solution.py:563
  72.1 0.8 collective-permute-done.11
  72.8 0.6 collective-permute-start.16
  73.4 2.0 %collective-permute-start.14 = (f32[4,8,8,256]{3,2,1,0:T(8,128)S(1)}, f32[4,8,8,256]{3,2,1,0:T(8,128)S(1)}, u32[]{:S(2)}, u32[]{:S(2)}) collective-permute-start(f32[4,8,8,256]{3,2,1,0:T(8,128)S(1)} %pad_maximum_fusion.refs_0_), channel_id=1, source_target_pairs={{0,1},{1,0},{2,3},{3,2},{4,5},{5,4},{6,7},{7,6},{8,9},{9,8},{10,11... | collective-permute-start | bytes 786440 | tf_op jit(solution)/shard_map/ppermute | solution.py:554
  75.4 0.0 collective-permute-start.18
  75.4 3.9 %collective-permute-done.16.refs_2_ = f32[4,8,8,256]{3,2,1,0:T(8,128)S(1)} collective-permute-done((f32[4,8,8,256]{3,2,1,0:T(8,128)S(1)}, f32[4,8,8,256]{3,2,1,0:T(8,128)S(1)}, u32[]{:S(2)}, u32[]{:S(2)}) %collective-permute-start.16) | collective-permute-done | bytes 262176 | tf_op jit(solution)/shard_map/ppermute | solution.py:554
  79.3 0.0 collective-permute-start.20
  79.3 0.8 collective-permute-done.14.refs_1_
  80.1 0.0 collective-permute-start.19
  80.1 1.8 %collective-permute-start.17 = (f32[2,8,8,256]{3,2,1,0:T(8,128)S(1)}, f32[2,8,8,256]{3,2,1,0:T(8,128)S(1)}, u32[]{:S(2)}, u32[]{:S(2)}) collective-permute-start(f32[2,8,8,256]{3,2,1,0:T(8,128)S(1)} %slice.153), channel_id=1, source_target_pairs={{0,1},{1,0},{2,3},{3,2},{4,5},{5,4},{6,7},{7,6},{8,9},{9,8},{10,11... | collective-permute-start | bytes 393224 | tf_op jit(solution)/shard_map/ppermute | solution.py:554
  81.9 0.9 collective-permute-start.15
  82.8 0.0 collective-permute-done.18.refs_3_
  82.8 0.0 collective-permute-done.20.refs_5_
  82.8 0.0 collective-permute-done.19.refs_4_
  82.8 1.9 %put_in_place.2.refs_4_ = f32[8,32,8,256]{3,2,1,0:T(8,128)} custom-call(s32[1,3]{1,0:T(1,128)S(1)} %add_bitcast_fusion.here_ref, f32[4,8,8,256]{3,2,1,0:T(8,128)S(1)} %pad_maximum_fusion.refs_0_, f32[4,8,8,256]{3,2,1,0:T(8,128)S(1)} %collective-permute-done.14.refs_1_, f32[4,8,8,256]{3,2,1,0:T(8,128)S(1)} %collective-permute-done.16.refs_2_, ...), custom_call_target="tpu_custom_call" | custom-call | bytes 4194304 | tf_op jit(solution)/shard_map/put_in_place/pallas_call | solution.py:518
  84.7 1.4 %collective-permute-done.17.refs_1_ = f32[2,8,8,256]{3,2,1,0:T(8,128)S(1)} collective-permute-done((f32[2,8,8,256]{3,2,1,0:T(8,128)S(1)}, f32[2,8,8,256]{3,2,1,0:T(8,128)S(1)}, u32[]{:S(2)}, u32[]{:S(2)}) %collective-permute-start.17) | collective-permute-done | bytes 131104 | tf_op jit(solution)/shard_map/ppermute | solution.py:554
  86.1 1.5 %collective-permute-done.15.refs_0_ = f32[2,8,8,256]{3,2,1,0:T(8,128)S(1)} collective-permute-done((f32[2,8,8,256]{3,2,1,0:T(8,128)S(1)}, f32[2,8,8,256]{3,2,1,0:T(8,128)S(1)}, u32[]{:S(2)}, u32[]{:S(2)}) %collective-permute-start.15) | collective-permute-done | bytes 131104 | tf_op jit(solution)/shard_map/ppermute | solution.py:554
  87.6 0.0 collective-permute-start.21
  87.6 0.5 collective-permute-start.22
  88.1 0.8 collective-permute-done.21.refs_2_
  89.0 0.2 collective-permute-done.22.refs_3_
  89.1 1.4 %put_in_place.3 = f32[8,32,8,256]{3,2,1,0:T(8,128)} custom-call(s32[1,3]{1,0:T(1,128)S(1)} %add_bitcast_fusion.here_ref, f32[2,8,8,256]{3,2,1,0:T(8,128)S(1)} %collective-permute-done.15.refs_0_, f32[2,8,8,256]{3,2,1,0:T(8,128)S(1)} %collective-permute-done.17.refs_1_, ...), custom_call_target="tpu_custom_call", output_to_operand_aliasing={{}: (5, {})} | custom-call | bytes 4194304 | tf_op jit(solution)/shard_map/put_in_place/pallas_call | solution.py:518
  (15 shorter events, 0.2 us)
Async XLA Ops:
  0.6 3.8 %copy-start.5 = (s32[4,2]{0,1:T(2,128)S(1)}, s32[4,2]{0,1:T(2,128)}, u32[]{:S(2)}) copy-start(s32[4,2]{0,1:T(2,128)} %param.13) | copy-start | bytes 100
  0.6 1.6 %copy-start = (f32[512,2,512]{2,1,0:T(2,128)S(1)}, f32[512,2,512]{2,1,0:T(2,128)}, u32[]{:S(2)}) copy-start(f32[512,2,512]{2,1,0:T(2,128)} %param.10) | copy-start | bytes 6291460
  2.2 2.5 %copy-start.1 = (f32[512,2,512]{2,1,0:T(2,128)S(1)}, f32[512,2,512]{2,1,0:T(2,128)}, u32[]{:S(2)}) copy-start(f32[512,2,512]{2,1,0:T(2,128)} %param.10) | copy-start | bytes 6291460
  2.2 2.5 %copy-start.4 = (f32[4,128,128]{2,1,0:T(8,128)S(1)}, f32[4,128,128]{2,1,0:T(8,128)}, u32[]{:S(2)}) copy-start(f32[4,128,128]{2,1,0:T(8,128)} %constant.93.clone.factor_ref) | copy-start | bytes 786436
  2.3 19.0 %collective-permute-start = (f32[2048,128]{1,0:T(8,128)S(1)}, f32[2048,128]{1,0:T(8,128)}, u32[]{:S(2)}, u32[]{:S(2)}) collective-permute-start(f32[2048,128]{1,0:T(8,128)S(1)} %first_rows.1), channel_id=1, source_target_pairs={{4,0},{8,4},{12,8},{16,12},{20,16},{24,20},{28,24},{5,1},{9,5},{13... | collective-permute-start | bytes 3145736 | tf_op jit(solution)/shard_map/ppermute | solution.py:22
  4.7 1.6 %copy-start.2 = (f32[4,2,256,256]{3,2,1,0:T(8,128)S(1)}, f32[4,2,256,256]{3,2,1,0:T(8,128)}, u32[]{:S(2)}) copy-start(f32[4,2,256,256]{3,2,1,0:T(8,128)} %probe_ref.1) | copy-start | bytes 6291460
  6.3 1.2 %copy-start.3 = (f32[4,256,256]{2,1,0:T(8,128)S(1)}, f32[4,256,256]{2,1,0:T(8,128)}, u32[]{:S(2)}) copy-start(f32[4,256,256]{2,1,0:T(8,128)} %diffraction_ref.1) | copy-start | bytes 3145732
  33.9 1.6 %collective-permute-start.1 = (f32[4,9,8,256]{3,2,1,0:T(8,128)S(1)}, f32[4,9,8,256]{3,2,1,0:T(8,128)S(1)}, u32[]{:S(2)}, u32[]{:S(2)}) collective-permute-start(f32[4,9,8,256]{3,2,1,0:T(8,128)S(1)} %get-tuple-element.71), channel_id=1, source_target_pairs={{0,4},{4,0},{8,12},{12,8},{16,20},{20,16},{24,28},{28,24},{1,5},{5... | collective-permute-start | bytes 884744 | tf_op jit(solution)/shard_map/ppermute | solution.py:558
  35.5 2.4 %collective-permute-start.2 = (f32[3,4,9,8,256]{4,3,2,1,0:T(8,128)S(1)}, f32[3,4,9,8,256]{4,3,2,1,0:T(8,128)S(1)}, u32[]{:S(2)}, u32[]{:S(2)}) collective-permute-start(f32[3,4,9,8,256]{4,3,2,1,0:T(8,128)S(1)} %get-tuple-element.72), channel_id=1, source_target_pairs={{0,4},{4,0},{8,12},{12,8},{16,20},{20,16},{24,28},{28,24},{1,5},{5... | collective-permute-start | bytes 2654216 | tf_op jit(solution)/shard_map/ppermute | solution.py:558
  35.7 6.2 %collective-permute-start.5 = (f32[2,9,8,256]{3,2,1,0:T(8,128)S(1)}, f32[2,9,8,256]{3,2,1,0:T(8,128)S(1)}, u32[]{:S(2)}, u32[]{:S(2)}) collective-permute-start(f32[2,9,8,256]{3,2,1,0:T(8,128)S(1)} %get-tuple-element.104), channel_id=1, source_target_pairs={{0,1},{1,0},{2,3},{3,2},{4,5},{5,4},{6,7},{7,6},{8,9},{9,8},{10,11... | collective-permute-start | bytes 442376 | tf_op jit(solution)/shard_map/ppermute | solution.py:554
  35.8 6.2 %collective-permute-start.3 = (f32[2,9,8,256]{3,2,1,0:T(8,128)S(1)}, f32[2,9,8,256]{3,2,1,0:T(8,128)S(1)}, u32[]{:S(2)}, u32[]{:S(2)}) collective-permute-start(f32[2,9,8,256]{3,2,1,0:T(8,128)S(1)} %get-tuple-element.105), channel_id=1, source_target_pairs={{0,2},{1,3},{2,0},{3,1},{4,6},{5,7},{6,4},{7,5},{8,10},{9,11},{10,... | collective-permute-start | bytes 442376 | tf_op jit(solution)/shard_map/ppermute | solution.py:554
  38.1 27.2 %collective-permute-start.10 = (f32[2048,128]{1,0:T(8,128)S(1)}, f32[2048,128]{1,0:T(8,128)S(1)}, u32[]{:S(2)}, u32[]{:S(2)}) collective-permute-start(f32[2048,128]{1,0:T(8,128)S(1)} %get-tuple-element.82), channel_id=1, source_target_pairs={{0,4},{4,8},{8,12},{12,16},{16,20},{20,24},{24,28},{1,5},{5,9},{9,... | collective-permute-start | bytes 3145736 | tf_op jit(solution)/shard_map/ppermute | solution.py:22
  42.0 6.8 %collective-permute-start.6 = (f32[4,9,8,256]{3,2,1,0:T(8,128)S(1)}, f32[4,9,8,256]{3,2,1,0:T(8,128)S(1)}, u32[]{:S(2)}, u32[]{:S(2)}) collective-permute-start(f32[4,9,8,256]{3,2,1,0:T(8,128)S(1)} %get-tuple-element.100), channel_id=1, source_target_pairs={{0,2},{1,3},{2,0},{3,1},{4,6},{5,7},{6,4},{7,5},{8,10},{9,11},{10,... | collective-permute-start | bytes 884744 | tf_op jit(solution)/shard_map/ppermute | solution.py:554
  42.4 6.7 %collective-permute-start.4 = (f32[4,9,8,256]{3,2,1,0:T(8,128)S(1)}, f32[4,9,8,256]{3,2,1,0:T(8,128)S(1)}, u32[]{:S(2)}, u32[]{:S(2)}) collective-permute-start(f32[4,9,8,256]{3,2,1,0:T(8,128)S(1)} %get-tuple-element.101), channel_id=1, source_target_pairs={{0,1},{1,0},{2,3},{3,2},{4,5},{5,4},{6,7},{7,6},{8,9},{9,8},{10,11... | collective-permute-start | bytes 884744 | tf_op jit(solution)/shard_map/ppermute | solution.py:554
  49.2 11.3 %collective-permute-start.9 = (f32[9,8,256]{2,1,0:T(8,128)S(1)}, f32[9,8,256]{2,1,0:T(8,128)S(1)}, u32[]{:S(2)}, u32[]{:S(2)}) collective-permute-start(f32[9,8,256]{2,1,0:T(8,128)S(1)} %get-tuple-element.96), channel_id=1, source_target_pairs={{0,24},{4,28},{8,0},{12,4},{16,8},{20,12},{24,16},{28,20},{1,25},{... | collective-permute-start | bytes 221192 | tf_op jit(solution)/shard_map/ppermute | solution.py:563
  53.5 10.3 %collective-permute-start.8 = (f32[9,8,256]{2,1,0:T(8,128)S(1)}, f32[9,8,256]{2,1,0:T(8,128)S(1)}, u32[]{:S(2)}, u32[]{:S(2)}) collective-permute-start(f32[9,8,256]{2,1,0:T(8,128)S(1)} %get-tuple-element.97), channel_id=1, source_target_pairs={{0,16},{4,20},{8,24},{12,28},{16,0},{20,4},{24,8},{28,12},{1,17},{... | collective-permute-start | bytes 221192 | tf_op jit(solution)/shard_map/ppermute | solution.py:563
  59.1 6.2 %collective-permute-start.7 = (f32[9,8,256]{2,1,0:T(8,128)S(1)}, f32[9,8,256]{2,1,0:T(8,128)S(1)}, u32[]{:S(2)}, u32[]{:S(2)}) collective-permute-start(f32[9,8,256]{2,1,0:T(8,128)S(1)} %get-tuple-element.98), channel_id=1, source_target_pairs={{0,8},{4,12},{8,16},{12,20},{16,24},{20,28},{24,0},{28,4},{1,9},{5... | collective-permute-start | bytes 221192 | tf_op jit(solution)/shard_map/ppermute | solution.py:563
  65.3 4.4 %collective-permute-start.13 = (f32[8,8,256]{2,1,0:T(8,128)S(1)}, f32[8,8,256]{2,1,0:T(8,128)S(1)}, u32[]{:S(2)}, u32[]{:S(2)}) collective-permute-start(f32[8,8,256]{2,1,0:T(8,128)S(1)} %divided.1), channel_id=1, source_target_pairs={{0,24},{4,28},{8,0},{12,4},{16,8},{20,12},{24,16},{28,20},{1,25},{... | collective-permute-start | bytes 196616 | tf_op jit(solution)/shard_map/ppermute | solution.py:563
  65.5 6.6 %collective-permute-start.12 = (f32[8,8,256]{2,1,0:T(8,128)S(1)}, f32[8,8,256]{2,1,0:T(8,128)S(1)}, u32[]{:S(2)}, u32[]{:S(2)}) collective-permute-start(f32[8,8,256]{2,1,0:T(8,128)S(1)} %divided.1), channel_id=1, source_target_pairs={{0,16},{4,20},{8,24},{12,28},{16,0},{20,4},{24,8},{28,12},{1,17},{... | collective-permute-start | bytes 196616 | tf_op jit(solution)/shard_map/ppermute | solution.py:563
  66.7 6.1 %collective-permute-start.11 = (f32[8,8,256]{2,1,0:T(8,128)S(1)}, f32[8,8,256]{2,1,0:T(8,128)S(1)}, u32[]{:S(2)}, u32[]{:S(2)}) collective-permute-start(f32[8,8,256]{2,1,0:T(8,128)S(1)} %divided.1), channel_id=1, source_target_pairs={{0,8},{4,12},{8,16},{12,20},{16,24},{20,28},{24,0},{28,4},{1,9},{5... | collective-permute-start | bytes 196616 | tf_op jit(solution)/shard_map/ppermute | solution.py:563
  72.8 6.4 %collective-permute-start.16 = (f32[4,8,8,256]{3,2,1,0:T(8,128)S(1)}, f32[4,8,8,256]{3,2,1,0:T(8,128)S(1)}, u32[]{:S(2)}, u32[]{:S(2)}) collective-permute-start(f32[4,8,8,256]{3,2,1,0:T(8,128)S(1)} %pad_maximum_fusion.refs_0_), channel_id=1, source_target_pairs={{0,2},{1,3},{2,0},{3,1},{4,6},{5,7},{6,4},{7,5},{8,10},{9,11},{10,... | collective-permute-start | bytes 786440 | tf_op jit(solution)/shard_map/ppermute | solution.py:554
  73.4 6.7 %collective-permute-start.14 = (f32[4,8,8,256]{3,2,1,0:T(8,128)S(1)}, f32[4,8,8,256]{3,2,1,0:T(8,128)S(1)}, u32[]{:S(2)}, u32[]{:S(2)}) collective-permute-start(f32[4,8,8,256]{3,2,1,0:T(8,128)S(1)} %pad_maximum_fusion.refs_0_), channel_id=1, source_target_pairs={{0,1},{1,0},{2,3},{3,2},{4,5},{5,4},{6,7},{7,6},{8,9},{9,8},{10,11... | collective-permute-start | bytes 786440 | tf_op jit(solution)/shard_map/ppermute | solution.py:554
  75.4 7.4 %collective-permute-start.18 = (f32[4,8,8,256]{3,2,1,0:T(8,128)S(1)}, f32[4,8,8,256]{3,2,1,0:T(8,128)S(1)}, u32[]{:S(2)}, u32[]{:S(2)}) collective-permute-start(f32[4,8,8,256]{3,2,1,0:T(8,128)S(1)} %pad_maximum_fusion.refs_0_), channel_id=1, source_target_pairs={{0,4},{4,0},{8,12},{12,8},{16,20},{20,16},{24,28},{28,24},{1,5},{5... | collective-permute-start | bytes 786440 | tf_op jit(solution)/shard_map/ppermute | solution.py:558
  79.3 3.5 %collective-permute-start.20 = (f32[4,8,8,256]{3,2,1,0:T(8,128)S(1)}, f32[4,8,8,256]{3,2,1,0:T(8,128)S(1)}, u32[]{:S(2)}, u32[]{:S(2)}) collective-permute-start(f32[4,8,8,256]{3,2,1,0:T(8,128)S(1)} %collective-permute-done.16.refs_2_), channel_id=1, source_target_pairs={{0,4},{4,0},{8,12},{12,8},{16,20},{20,16},{24,28},{28,24},{1,5},{5... | collective-permute-start | bytes 786440 | tf_op jit(solution)/shard_map/ppermute | solution.py:558
  80.1 2.7 %collective-permute-start.19 = (f32[4,8,8,256]{3,2,1,0:T(8,128)S(1)}, f32[4,8,8,256]{3,2,1,0:T(8,128)S(1)}, u32[]{:S(2)}, u32[]{:S(2)}) collective-permute-start(f32[4,8,8,256]{3,2,1,0:T(8,128)S(1)} %collective-permute-done.14.refs_1_), channel_id=1, source_target_pairs={{0,4},{4,0},{8,12},{12,8},{16,20},{20,16},{24,28},{28,24},{1,5},{5... | collective-permute-start | bytes 786440 | tf_op jit(solution)/shard_map/ppermute | solution.py:558
  80.1 6.0 %collective-permute-start.17 = (f32[2,8,8,256]{3,2,1,0:T(8,128)S(1)}, f32[2,8,8,256]{3,2,1,0:T(8,128)S(1)}, u32[]{:S(2)}, u32[]{:S(2)}) collective-permute-start(f32[2,8,8,256]{3,2,1,0:T(8,128)S(1)} %slice.153), channel_id=1, source_target_pairs={{0,1},{1,0},{2,3},{3,2},{4,5},{5,4},{6,7},{7,6},{8,9},{9,8},{10,11... | collective-permute-start | bytes 393224 | tf_op jit(solution)/shard_map/ppermute | solution.py:554
  81.9 5.7 %collective-permute-start.15 = (f32[2,8,8,256]{3,2,1,0:T(8,128)S(1)}, f32[2,8,8,256]{3,2,1,0:T(8,128)S(1)}, u32[]{:S(2)}, u32[]{:S(2)}) collective-permute-start(f32[2,8,8,256]{3,2,1,0:T(8,128)S(1)} %slice.152), channel_id=1, source_target_pairs={{0,2},{1,3},{2,0},{3,1},{4,6},{5,7},{6,4},{7,5},{8,10},{9,11},{10,... | collective-permute-start | bytes 393224 | tf_op jit(solution)/shard_map/ppermute | solution.py:554
  87.6 1.3 %collective-permute-start.21 = (f32[2,8,8,256]{3,2,1,0:T(8,128)S(1)}, f32[2,8,8,256]{3,2,1,0:T(8,128)S(1)}, u32[]{:S(2)}, u32[]{:S(2)}) collective-permute-start(f32[2,8,8,256]{3,2,1,0:T(8,128)S(1)} %collective-permute-done.15.refs_0_), channel_id=1, source_target_pairs={{0,4},{4,0},{8,12},{12,8},{16,20},{20,16},{24,28},{28,24},{1,5},{5... | collective-permute-start | bytes 393224 | tf_op jit(solution)/shard_map/ppermute | solution.py:558
  87.6 1.5 %collective-permute-start.22 = (f32[2,8,8,256]{3,2,1,0:T(8,128)S(1)}, f32[2,8,8,256]{3,2,1,0:T(8,128)S(1)}, u32[]{:S(2)}, u32[]{:S(2)}) collective-permute-start(f32[2,8,8,256]{3,2,1,0:T(8,128)S(1)} %collective-permute-done.17.refs_1_), channel_id=1, source_target_pairs={{0,4},{4,0},{8,12},{12,8},{16,20},{20,16},{24,28},{28,24},{1,5},{5... | collective-permute-start | bytes 393224 | tf_op jit(solution)/shard_map/ppermute | solution.py:558
where the time goes:
time: 92.3 us; the launch traced here: 90.7 us
  Pallas kernels  32.2 us (35%)
  waiting for transfers between devices  27.6 us (30%)
  starting transfers between devices  24.2 us (26%)
  local copies, waits for them, and re-layouts  4.59 us (5%)
  between operations  1.65 us (2%)
    pallas_call x1, Pallas kernels, gradient_step(): pl.pallas_call(first_kernel, out_shape=(shape(tile.shape, f32), shape(til...  13.9 us
    ppermute x8, waiting for transfers between devices, across(): lax.ppermute(block, 'group', [(i, i ^ hop) for i in range(lax.axis_size('...  12.8 us
    pallas_call x1, Pallas kernels, gradient_step(): pl.pallas_call(second_kernel, out_shape=(shape((tile.shape[0] + halo.shap...  12.5 us
    ppermute x6, starting transfers between devices, up_layers(): lax.ppermute(block, 'region', [(i, (i + 2 * step) % regions) for i in ran...  12.4 us
    ppermute x6, waiting for transfers between devices, up_layers(): lax.ppermute(block, 'region', [(i, (i + 2 * step) % regions) for i in ran...  10.1 us
    ppermute x8, starting transfers between devices, across(): lax.ppermute(block, 'group', [(i, i ^ hop) for i in range(lax.axis_size('...  7.39 us
    ppermute x7, waiting for transfers between devices, from_partner(): lax.ppermute(block, 'region', [(i, i ^ 1) for i in range(lax.axis_size('r...  4.66 us
    unnamed x13, local copies, waits for them, and re-layouts  4.51 us
  transfers between devices with their start and end apart: 23, of which 18 were waited for; matrix products, arithmetic and copies ran while one was open for 1% of the time, Pallas kernels for 20%

commit v1 on v0

--- a/solution.py
+++ b/solution.py
@@ -11,6 +11,7 @@
 
 LANES = 128
 SUBLANES = 8
+PITCH = 9
 ROWS = 32
 STREAM = 2
 EPSILON = 1e-06
@@ -117,6 +118,16 @@
 
 def beside(real, imag):
     return jnp.concatenate([real, imag], axis=1)
+
+
+def spread(source, target, first, rows):
+    for row in range(rows):
+        target[pl.ds((first + row) * PITCH, SUBLANES), :] = source[pl.ds(row * SUBLANES, SUBLANES), :]
+
+
+def gathered(source, first, target, rows):
+    for row in range(rows):
+        target[pl.ds(row * SUBLANES, SUBLANES), :] = source[pl.ds((first + row) * PITCH, SUBLANES), :]
 
 
 def all_slots(
@@ -157,8 +168,8 @@
         last = per_row // 2 - 1
 
         def strided(block, part):
-            at = row * per_row + jnp.minimum(first + block, last) * 2 + part
-            return pl.ds(at, side, stride=per_row)
+            at = row * PITCH + jnp.minimum(first + block, last) * 2 + part
+            return pl.ds(at, side, stride=PITCH)
 
         for part in range(2):
             rolled = [
@@ -281,6 +292,7 @@
     probe_out,
     table_out,
     scale_out,
+    extended,
     window,
     terms,
     result,
@@ -311,8 +323,10 @@
 
     lax.fori_loop(0, count_ref[0, 0], order, 0)
     copy.wait()
+    rows = tile_out.shape[0] // SUBLANES
+    spread(tile_out, extended, 0, rows)
     all_slots(
-        True, tile_out.shape[0] // SUBLANES, place_ref, count_ref, probe_ref, table_out, tile_out,
+        True, rows, place_ref, count_ref, probe_ref, table_out, extended,
         gradient, sums, power, measured, window, terms, result, back,
     )
 
@@ -343,17 +357,18 @@
     back,
 ):
     modes = probe_ref.shape[0]
-    tile_rows, halo_rows, chunks = tile_ref.shape[0], halo_ref.shape[0], sums.shape[0]
-    extended[pl.ds(0, tile_rows), :] = tile_ref[...]
-    extended[pl.ds(tile_rows, halo_rows), :] = halo_ref[...]
-    gradient[pl.ds(0, tile_rows), :] = gradient_ref[...]
-    gradient[pl.ds(tile_rows, halo_rows), :] = jnp.zeros((halo_rows, LANES), jnp.float32)
+    tile_rows, halo_rows = tile_ref.shape[0] // SUBLANES, halo_ref.shape[0] // SUBLANES
+    chunks = sums.shape[0]
+    spread(tile_ref, extended, 0, tile_rows)
+    spread(halo_ref, extended, tile_rows, halo_rows)
+    gradient[pl.ds(0, tile_rows * PITCH), :] = gradient_ref[...]
+    gradient[pl.ds(tile_rows * PITCH, halo_rows * PITCH), :] = jnp.zeros((halo_rows * PITCH, LANES), jnp.float32)
     sums[...] = sums_ref[...]
     all_slots(
-        False, tile_rows // SUBLANES, place_ref, count_ref, probe_ref, table_ref, extended,
+        False, tile_rows, place_ref, count_ref, probe_ref, table_ref, extended,
         gradient, sums, power, measured, window, terms, result, back,
     )
-    spill_out[...] = gradient[pl.ds(tile_rows, halo_rows), :]
+    gathered(gradient, tile_rows, spill_out, halo_rows)
     core, group, layer = here_ref[0, 0], here_ref[0, 1], here_ref[0, 2]
     groups, layers = mine_out.shape[0], mine_out.shape[1]
     for hop in range(groups):
@@ -378,6 +393,7 @@
     smem = pl.BlockSpec(memory_space=pltpu.SMEM)
     vmem = pl.BlockSpec(memory_space=pltpu.VMEM)
     chunk = (planes, SUBLANES, side)
+    tile_rows, halo_rows = tile.shape[0] // SUBLANES, halo.shape[0] // SUBLANES
     products = 3 * 16 * modes * diffraction.shape[0] * side**3 // 2
     work = [
         pltpu.VMEM((2, side, side), f32),
@@ -391,7 +407,7 @@
         first_kernel,
         out_shape=(
             shape(tile.shape, f32),
-            shape(tile.shape, f32),
+            shape((tile_rows * PITCH, LANES), f32),
             shape((chunks, *chunk), f32),
             shape(diffraction.shape, f32),
             shape((side, side), f32),
@@ -401,7 +417,7 @@
         ),
         in_specs=[smem, smem, pl.BlockSpec(memory_space=pl.ANY), vmem, vmem, vmem],
         out_specs=(vmem,) * 8,
-        scratch_shapes=work + [pltpu.SemaphoreType.DMA],
+        scratch_shapes=[pltpu.VMEM((tile_rows * PITCH, LANES), f32)] + work + [pltpu.SemaphoreType.DMA],
         compiler_params=pltpu.CompilerParams(vmem_limit_bytes=28 * 1024 * 1024),
         cost_estimate=cost,
         name="slots_inside",
@@ -409,7 +425,7 @@
     gradient, *rest = pl.pallas_call(
         second_kernel,
         out_shape=(
-            shape((tile.shape[0] + halo.shape[0], LANES), f32),
+            shape(((tile_rows + halo_rows) * PITCH, LANES), f32),
             shape(halo.shape, f32),
             shape((groups, layers, *chunk), f32),
             shape((groups - 1, layers, *chunk), f32),
@@ -419,7 +435,7 @@
         in_specs=[smem, smem, smem] + [vmem] * 8,
         out_specs=(vmem,) * 6,
         scratch_shapes=[
-            pltpu.VMEM((tile.shape[0] + halo.shape[0], LANES), f32),
+            pltpu.VMEM(((tile_rows + halo_rows) * PITCH, LANES), f32),
             pltpu.VMEM((chunks, *chunk), f32),
         ]
         + work,
@@ -437,7 +453,8 @@
     copies = []
     for part in range(4):
         at = pl.ds(part * step, step)
-        rows[at, :] = tile_ref[at, :] - gradient_ref[at, :] * scale
+        gathered(gradient_ref, part * step // SUBLANES, rows.at[at], step // SUBLANES)
+        rows[at, :] = tile_ref[at, :] - rows[at, :] * scale
         copies.append(pltpu.make_async_copy(rows.at[at], out_ref.at[at], semaphores.at[part]))
         copies[-1].start()
     top_ref[...] = rows[pl.ds(0, top_ref.shape[0]), :]

time: 92.3 us -> 91.2 us (0.988); the launches traced: 90.7 us -> 90.9 us
  starting transfers between devices: 24.2 us -> 36.3 us
  Pallas kernels: 32.2 us -> 21 us
    ppermute x7, starting transfers between devices: 0.73 us -> 13.3 us  [from_partner(): lax.ppermute(block, 'region', [(i, i ^ 1) for i in range(lax.axis_size('r...]
    pallas_call x2, Pallas kernels: 26.3 us -> 15.1 us  [the longest x1 13 us: gradient_step(): pl.pallas_call(first_kernel, out_shape=(shape(tile.shape, f32), shape((ti...]
    ppermute x6, waiting for transfers between devices: 10.1 us -> 8.72 us  [up_layers(): lax.ppermute(block, 'region', [(i, (i + 2 * step) % regions) for i in ran...]
    ppermute x8, waiting for transfers between devices: 12.8 us -> 14.1 us  [across(): lax.ppermute(block, 'group', [(i, i ^ hop) for i in range(lax.axis_size('...]
  transfers between devices with their start and end apart: 23 -> 23, of which waited for: 18 -> 16; matrix products, arithmetic and copies ran while one was open for 1% -> 1% of each run, Pallas kernels for 20% -> 19%
where the time goes in v1:
time: 91.2 us; the launch traced here: 90.9 us
  starting transfers between devices  36.3 us (40%)
  waiting for transfers between devices  26.9 us (29%)
  Pallas kernels  21 us (23%)
  local copies, waits for them, and re-layouts  4.59 us (5%)
  between operations  1.64 us (2%)
    ppermute x8, waiting for transfers between devices, across(): lax.ppermute(block, 'group', [(i, i ^ hop) for i in range(lax.axis_size('...  14.1 us
    ppermute x7, starting transfers between devices, from_partner(): lax.ppermute(block, 'region', [(i, i ^ 1) for i in range(lax.axis_size('r...  13.3 us
    pallas_call x1, Pallas kernels, gradient_step(): pl.pallas_call(first_kernel, out_shape=(shape(tile.shape, f32), shape((ti...  13 us
    ppermute x6, starting transfers between devices, up_layers(): lax.ppermute(block, 'region', [(i, (i + 2 * step) % regions) for i in ran...  12.2 us
    ppermute x6, waiting for transfers between devices, up_layers(): lax.ppermute(block, 'region', [(i, (i + 2 * step) % regions) for i in ran...  8.72 us
    ppermute x8, starting transfers between devices, across(): lax.ppermute(block, 'group', [(i, i ^ hop) for i in range(lax.axis_size('...  6.91 us
    unnamed x13, local copies, waits for them, and re-layouts  4.51 us
    ppermute x7, waiting for transfers between devices, from_partner(): lax.ppermute(block, 'region', [(i, i ^ 1) for i in range(lax.axis_size('r...  4.07 us
  transfers between devices with their start and end apart: 23, of which 16 were waited for; matrix products, arithmetic and copies ran while one was open for 1% of the time, Pallas kernels for 19%

profile of v1, /device:TPU:0, one launch (start us, length us, event | category | flops | bytes accessed | tf_op | source)
XLA Modules:
  0.0 90.9 jit_solution(5758024194636232862)
XLA Ops:
  0.6 0.0 copy-start.5
  0.6 0.0 copy-start
  0.6 1.6 %copy-done = f32[512,2,512]{2,1,0:T(2,128)S(1)} copy-done((f32[512,2,512]{2,1,0:T(2,128)S(1)}, f32[512,2,512]{2,1,0:T(2,128)}, u32[]{:S(2)}) %copy-start) | copy-done | bytes 2097176
  2.2 0.1 first_rows.1
  2.3 1.4 %collective-permute-start = (f32[2048,128]{1,0:T(8,128)S(1)}, f32[2048,128]{1,0:T(8,128)}, u32[]{:S(2)}, u32[]{:S(2)}) collective-permute-start(f32[2048,128]{1,0:T(8,128)S(1)} %first_rows.1), channel_id=1, source_target_pairs={{4,0},{8,4},{12,8},{16,12},{20,16},{24,20},{28,24},{5,1},{9,5},{13... | collective-permute-start | bytes 3145736 | tf_op jit(solution)/shard_map/ppermute | solution.py:23
  4.4 0.1 copy.10
  4.5 0.1 pad_add_fusion
  4.6 0.1 add_bitcast_fusion.here_ref
  4.7 0.0 copy-done.4
  4.7 1.6 %copy-done.2 = f32[4,2,256,256]{3,2,1,0:T(8,128)S(1)} copy-done((f32[4,2,256,256]{3,2,1,0:T(8,128)S(1)}, f32[4,2,256,256]{3,2,1,0:T(8,128)}, u32[]{:S(2)}) %copy-start.2) | copy-done | bytes 2097176
  6.3 1.2 %copy-done.3 = f32[4,256,256]{2,1,0:T(8,128)S(1)} copy-done((f32[4,256,256]{2,1,0:T(8,128)S(1)}, f32[4,256,256]{2,1,0:T(8,128)}, u32[]{:S(2)}) %copy-start.3) | copy-done | bytes 1048600
  7.5 13.0 %slots_inside.1 = (f32[4096,128]{1,0:T(8,128)S(1)}, f32[4608,128]{1,0:T(8,128)S(1)}, f32[32,9,8,256]{3,2,1,0:T(8,128)S(1)}, f32[4,256,256]{2,1,0:T(8,128)S(1)}, ...) custom-call(s32[4,2]{1,0:T(4,128)S(1)} %broadcast_subtract_fusion.pl, ...), custom_call_target="tpu_custom_call" | custom-call | flops 12884901888 | bytes 16777216 | tf_op jit(solution)/shard_map/slots_inside/pallas_call | solution.py:406
  20.5 0.0 collective-permute-done.halo_ref
  20.5 2.1 %slots_across.1 = (f32[6912,128]{1,0:T(8,128)S(1)}, f32[2048,128]{1,0:T(8,128)S(1)}, f32[4,4,9,8,256]{4,3,2,1,0:T(8,128)S(1)}, f32[3,4,9,8,256]{4,3,2,1,0:T(8,12...) custom-call(s32[4,2]{1,0:T(4,128)S(1)} %broadcast_subtract_fusion.place_ref, s32[1,1]{1,0:T(1,128)S(6)} %copy.17.count_ref, ...), custom_call_target="tpu_custom_call" | custom-call | flops 12884901888 | bytes 16777216 | tf_op jit(solution)/shard_map/slots_across/pallas_call | solution.py:425
  22.6 12.4 %collective-permute-start.1 = (f32[4,9,8,256]{3,2,1,0:T(8,128)S(1)}, f32[4,9,8,256]{3,2,1,0:T(8,128)S(1)}, u32[]{:S(2)}, u32[]{:S(2)}) collective-permute-start(f32[4,9,8,256]{3,2,1,0:T(8,128)S(1)} %get-tuple-element.71), channel_id=1, source_target_pairs={{0,4},{4,0},{8,12},{12,8},{16,20},{20,16},{24,28},{28,24},{1,5},{5... | collective-permute-start | bytes 884744 | tf_op jit(solution)/shard_map/ppermute | solution.py:575
  35.0 1.2 %collective-permute-done.1 = f32[4,9,8,256]{3,2,1,0:T(8,128)S(1)} collective-permute-done((f32[4,9,8,256]{3,2,1,0:T(8,128)S(1)}, f32[4,9,8,256]{3,2,1,0:T(8,128)S(1)}, u32[]{:S(2)}, u32[]{:S(2)}) %collective-permute-start.1) | collective-permute-done | bytes 294944 | tf_op jit(solution)/shard_map/ppermute | solution.py:575
  36.2 0.4 collective-permute-start.2
  36.6 0.1 collective-permute-start.5
  36.7 0.1 collective-permute-start.3
  36.8 1.8 %collective-permute-done.2 = f32[3,4,9,8,256]{4,3,2,1,0:T(8,128)S(1)} collective-permute-done((f32[3,4,9,8,256]{4,3,2,1,0:T(8,128)S(1)}, f32[3,4,9,8,256]{4,3,2,1,0:T(8,128)S(1)}, u32[]{:S(2)}, u32[]{:S(2)}) %collective-permute-start.2) | collective-permute-done | bytes 884768 | tf_op jit(solution)/shard_map/ppermute | solution.py:575
  38.6 0.1 slice_add_fusion
  38.7 2.5 %collective-permute-start.10 = (f32[2048,128]{1,0:T(8,128)S(1)}, f32[2048,128]{1,0:T(8,128)S(1)}, u32[]{:S(2)}, u32[]{:S(2)}) collective-permute-start(f32[2048,128]{1,0:T(8,128)S(1)} %get-tuple-element.82), channel_id=1, source_target_pairs={{0,4},{4,8},{8,12},{12,16},{16,20},{20,24},{24,28},{1,5},{5,9},{9,... | collective-permute-start | bytes 3145736 | tf_op jit(solution)/shard_map/ppermute | solution.py:23
  41.3 1.3 %collective-permute-done.5 = f32[2,9,8,256]{3,2,1,0:T(8,128)S(1)} collective-permute-done((f32[2,9,8,256]{3,2,1,0:T(8,128)S(1)}, f32[2,9,8,256]{3,2,1,0:T(8,128)S(1)}, u32[]{:S(2)}, u32[]{:S(2)}) %collective-permute-start.5) | collective-permute-done | bytes 147488 | tf_op jit(solution)/shard_map/ppermute | solution.py:571
  42.6 0.1 collective-permute-done.3
  42.7 0.4 collective-permute-start.6
  43.1 1.7 %collective-permute-start.4 = (f32[4,9,8,256]{3,2,1,0:T(8,128)S(1)}, f32[4,9,8,256]{3,2,1,0:T(8,128)S(1)}, u32[]{:S(2)}, u32[]{:S(2)}) collective-permute-start(f32[4,9,8,256]{3,2,1,0:T(8,128)S(1)} %get-tuple-element.101), channel_id=1, source_target_pairs={{0,1},{1,0},{2,3},{3,2},{4,5},{5,4},{6,7},{7,6},{8,9},{9,8},{10,11... | collective-permute-start | bytes 884744 | tf_op jit(solution)/shard_map/ppermute | solution.py:571
  44.7 1.4 %written.1 = (f32[4096,128]{1,0:T(8,128)}, f32[2048,128]{1,0:T(8,128)S(1)}) custom-call(f32[4096,128]{1,0:T(8,128)S(1)} %get-tuple-element.61.tile_ref, f32[6912,128]{1,0:T(8,128)S(1)} %get-tuple-element.76.gradient_ref, f32[1,128]{1,0:T(1,128)S(1)} %get-tuple-element.77.scale_ref), custom_call_target="tpu_custom_call" | custom-call | bytes 4194304 | tf_op jit(solution)/shard_map/written/pallas_call | solution.py:467
  46.2 5.2 %collective-permute-done.6 = f32[4,9,8,256]{3,2,1,0:T(8,128)S(1)} collective-permute-done((f32[4,9,8,256]{3,2,1,0:T(8,128)S(1)}, f32[4,9,8,256]{3,2,1,0:T(8,128)S(1)}, u32[]{:S(2)}, u32[]{:S(2)}) %collective-permute-start.6) | collective-permute-done | bytes 294944 | tf_op jit(solution)/shard_map/ppermute | solution.py:571
  51.4 0.0 collective-permute-done.4
  51.4 0.1 fusion.5
  51.4 7.8 %collective-permute-start.9 = (f32[9,8,256]{2,1,0:T(8,128)S(1)}, f32[9,8,256]{2,1,0:T(8,128)S(1)}, u32[]{:S(2)}, u32[]{:S(2)}) collective-permute-start(f32[9,8,256]{2,1,0:T(8,128)S(1)} %get-tuple-element.96), channel_id=1, source_target_pairs={{0,24},{4,28},{8,0},{12,4},{16,8},{20,12},{24,16},{28,20},{1,25},{... | collective-permute-start | bytes 221192 | tf_op jit(solution)/shard_map/ppermute | solution.py:580
  59.2 0.0 collective-permute-start.8
  59.2 0.9 collective-permute-start.7
  60.1 1.1 %collective-permute-done.9.refs_3_ = f32[9,8,256]{2,1,0:T(8,128)S(1)} collective-permute-done((f32[9,8,256]{2,1,0:T(8,128)S(1)}, f32[9,8,256]{2,1,0:T(8,128)S(1)}, u32[]{:S(2)}, u32[]{:S(2)}) %collective-permute-start.9) | collective-permute-done | bytes 73760 | tf_op jit(solution)/shard_map/ppermute | solution.py:580
  61.2 3.4 %collective-permute-done.8.refs_2_ = f32[9,8,256]{2,1,0:T(8,128)S(1)} collective-permute-done((f32[9,8,256]{2,1,0:T(8,128)S(1)}, f32[9,8,256]{2,1,0:T(8,128)S(1)}, u32[]{:S(2)}, u32[]{:S(2)}) %collective-permute-start.8) | collective-permute-done | bytes 73760 | tf_op jit(solution)/shard_map/ppermute | solution.py:580
  64.6 0.8 collective-permute-done.7.refs_1_
  65.4 0.0 collective-permute-done.10.arrived_ref
  65.4 1.6 %collective-permute-start.13 = (f32[8,8,256]{2,1,0:T(8,128)S(1)}, f32[8,8,256]{2,1,0:T(8,128)S(1)}, u32[]{:S(2)}, u32[]{:S(2)}) collective-permute-start(f32[8,8,256]{2,1,0:T(8,128)S(1)} %divided.1), channel_id=1, source_target_pairs={{0,24},{4,28},{8,0},{12,4},{16,8},{20,12},{24,16},{28,20},{1,25},{... | collective-permute-start | bytes 196616 | tf_op jit(solution)/shard_map/ppermute | solution.py:580
  67.0 0.0 collective-permute-start.12
  67.0 1.9 %collective-permute-start.11 = (f32[8,8,256]{2,1,0:T(8,128)S(1)}, f32[8,8,256]{2,1,0:T(8,128)S(1)}, u32[]{:S(2)}, u32[]{:S(2)}) collective-permute-start(f32[8,8,256]{2,1,0:T(8,128)S(1)} %divided.1), channel_id=1, source_target_pairs={{0,8},{4,12},{8,16},{12,20},{16,24},{20,28},{24,0},{28,4},{1,9},{5... | collective-permute-start | bytes 196616 | tf_op jit(solution)/shard_map/ppermute | solution.py:580
  68.9 1.1 %with_top.1 = f32[4096,128]{1,0:T(8,128)} custom-call(f32[4096,128]{1,0:T(8,128)} %get-tuple-element.86.held_ref, f32[2048,128]{1,0:T(8,128)S(1)} %get-tuple-element.87.top_ref, f32[2048,128]{1,0:T(8,128)S(1)} %collective-permute-done.10.arrived_ref, f32[1,128]{1,0:T(1,128)S(1)} %get-tuple-element.77.scale_ref), custom_call_target="tpu_custom_call", output_to_operand_aliasing={{}: (0, {})} | custom-call | bytes 2097152 | tf_op jit(solution)/shard_map/with_top/pallas_call | solution.py:557
  70.0 0.4 collective-permute-done.13
  70.4 3.1 %collective-permute-done.12 = f32[8,8,256]{2,1,0:T(8,128)S(1)} collective-permute-done((f32[8,8,256]{2,1,0:T(8,128)S(1)}, f32[8,8,256]{2,1,0:T(8,128)S(1)}, u32[]{:S(2)}, u32[]{:S(2)}) %collective-permute-start.12) | collective-permute-done | bytes 65568 | tf_op jit(solution)/shard_map/ppermute | solution.py:580
  73.5 0.0 collective-permute-done.11
  73.5 1.1 %collective-permute-start.16 = (f32[4,8,8,256]{3,2,1,0:T(8,128)S(1)}, f32[4,8,8,256]{3,2,1,0:T(8,128)S(1)}, u32[]{:S(2)}, u32[]{:S(2)}) collective-permute-start(f32[4,8,8,256]{3,2,1,0:T(8,128)S(1)} %pad_maximum_fusion.refs_0_), channel_id=1, source_target_pairs={{0,2},{1,3},{2,0},{3,1},{4,6},{5,7},{6,4},{7,5},{8,10},{9,11},{10,... | collective-permute-start | bytes 786440 | tf_op jit(solution)/shard_map/ppermute | solution.py:571
  74.6 1.0 %collective-permute-start.14 = (f32[4,8,8,256]{3,2,1,0:T(8,128)S(1)}, f32[4,8,8,256]{3,2,1,0:T(8,128)S(1)}, u32[]{:S(2)}, u32[]{:S(2)}) collective-permute-start(f32[4,8,8,256]{3,2,1,0:T(8,128)S(1)} %pad_maximum_fusion.refs_0_), channel_id=1, source_target_pairs={{0,1},{1,0},{2,3},{3,2},{4,5},{5,4},{6,7},{7,6},{8,9},{9,8},{10,11... | collective-permute-start | bytes 786440 | tf_op jit(solution)/shard_map/ppermute | solution.py:571
  75.6 0.0 collective-permute-start.18
  75.6 4.3 %collective-permute-done.16.refs_2_ = f32[4,8,8,256]{3,2,1,0:T(8,128)S(1)} collective-permute-done((f32[4,8,8,256]{3,2,1,0:T(8,128)S(1)}, f32[4,8,8,256]{3,2,1,0:T(8,128)S(1)}, u32[]{:S(2)}, u32[]{:S(2)}) %collective-permute-start.16) | collective-permute-done | bytes 262176 | tf_op jit(solution)/shard_map/ppermute | solution.py:571
  80.0 0.0 collective-permute-start.20
  80.0 1.0 %collective-permute-done.14.refs_1_ = f32[4,8,8,256]{3,2,1,0:T(8,128)S(1)} collective-permute-done((f32[4,8,8,256]{3,2,1,0:T(8,128)S(1)}, f32[4,8,8,256]{3,2,1,0:T(8,128)S(1)}, u32[]{:S(2)}, u32[]{:S(2)}) %collective-permute-start.14) | collective-permute-done | bytes 262176 | tf_op jit(solution)/shard_map/ppermute | solution.py:571
  81.0 0.0 collective-permute-start.19
  81.0 1.1 %collective-permute-start.17 = (f32[2,8,8,256]{3,2,1,0:T(8,128)S(1)}, f32[2,8,8,256]{3,2,1,0:T(8,128)S(1)}, u32[]{:S(2)}, u32[]{:S(2)}) collective-permute-start(f32[2,8,8,256]{3,2,1,0:T(8,128)S(1)} %slice.153), channel_id=1, source_target_pairs={{0,1},{1,0},{2,3},{3,2},{4,5},{5,4},{6,7},{7,6},{8,9},{9,8},{10,11... | collective-permute-start | bytes 393224 | tf_op jit(solution)/shard_map/ppermute | solution.py:571
  82.1 1.6 %collective-permute-start.15 = (f32[2,8,8,256]{3,2,1,0:T(8,128)S(1)}, f32[2,8,8,256]{3,2,1,0:T(8,128)S(1)}, u32[]{:S(2)}, u32[]{:S(2)}) collective-permute-start(f32[2,8,8,256]{3,2,1,0:T(8,128)S(1)} %slice.152), channel_id=1, source_target_pairs={{0,2},{1,3},{2,0},{3,1},{4,6},{5,7},{6,4},{7,5},{8,10},{9,11},{10,... | collective-permute-start | bytes 393224 | tf_op jit(solution)/shard_map/ppermute | solution.py:571
  83.7 0.0 collective-permute-done.18.refs_3_
  83.7 0.0 collective-permute-done.20.refs_5_
  83.7 0.0 collective-permute-done.19.refs_4_
  83.7 1.9 %put_in_place.2.refs_4_ = f32[8,32,8,256]{3,2,1,0:T(8,128)} custom-call(s32[1,3]{1,0:T(1,128)S(1)} %add_bitcast_fusion.here_ref, f32[4,8,8,256]{3,2,1,0:T(8,128)S(1)} %pad_maximum_fusion.refs_0_, f32[4,8,8,256]{3,2,1,0:T(8,128)S(1)} %collective-permute-done.14.refs_1_, f32[4,8,8,256]{3,2,1,0:T(8,128)S(1)} %collective-permute-done.16.refs_2_, ...), custom_call_target="tpu_custom_call" | custom-call | bytes 4194304 | tf_op jit(solution)/shard_map/put_in_place/pallas_call | solution.py:535
  85.6 1.4 %collective-permute-done.17.refs_1_ = f32[2,8,8,256]{3,2,1,0:T(8,128)S(1)} collective-permute-done((f32[2,8,8,256]{3,2,1,0:T(8,128)S(1)}, f32[2,8,8,256]{3,2,1,0:T(8,128)S(1)}, u32[]{:S(2)}, u32[]{:S(2)}) %collective-permute-start.17) | collective-permute-done | bytes 131104 | tf_op jit(solution)/shard_map/ppermute | solution.py:571
  87.0 0.8 collective-permute-done.15.refs_0_
  87.8 0.0 collective-permute-start.21
  87.8 0.5 collective-permute-start.22
  88.3 0.8 collective-permute-done.21.refs_2_
  89.1 0.2 collective-permute-done.22.refs_3_
  89.3 1.4 %put_in_place.3 = f32[8,32,8,256]{3,2,1,0:T(8,128)} custom-call(s32[1,3]{1,0:T(1,128)S(1)} %add_bitcast_fusion.here_ref, f32[2,8,8,256]{3,2,1,0:T(8,128)S(1)} %collective-permute-done.15.refs_0_, f32[2,8,8,256]{3,2,1,0:T(8,128)S(1)} %collective-permute-done.17.refs_1_, ...), custom_call_target="tpu_custom_call", output_to_operand_aliasing={{}: (5, {})} | custom-call | bytes 4194304 | tf_op jit(solution)/shard_map/put_in_place/pallas_call | solution.py:535
  (15 shorter events, 0.2 us)
Async XLA Ops:
  0.6 3.8 %copy-start.5 = (s32[4,2]{0,1:T(2,128)S(1)}, s32[4,2]{0,1:T(2,128)}, u32[]{:S(2)}) copy-start(s32[4,2]{0,1:T(2,128)} %param.13) | copy-start | bytes 100
  0.6 1.6 %copy-start = (f32[512,2,512]{2,1,0:T(2,128)S(1)}, f32[512,2,512]{2,1,0:T(2,128)}, u32[]{:S(2)}) copy-start(f32[512,2,512]{2,1,0:T(2,128)} %param.10) | copy-start | bytes 6291460
  2.2 2.5 %copy-start.1 = (f32[512,2,512]{2,1,0:T(2,128)S(1)}, f32[512,2,512]{2,1,0:T(2,128)}, u32[]{:S(2)}) copy-start(f32[512,2,512]{2,1,0:T(2,128)} %param.10) | copy-start | bytes 6291460
  2.2 2.5 %copy-start.4 = (f32[4,128,128]{2,1,0:T(8,128)S(1)}, f32[4,128,128]{2,1,0:T(8,128)}, u32[]{:S(2)}) copy-start(f32[4,128,128]{2,1,0:T(8,128)} %constant.93.clone.factor_ref) | copy-start | bytes 786436
  2.3 18.2 %collective-permute-start = (f32[2048,128]{1,0:T(8,128)S(1)}, f32[2048,128]{1,0:T(8,128)}, u32[]{:S(2)}, u32[]{:S(2)}) collective-permute-start(f32[2048,128]{1,0:T(8,128)S(1)} %first_rows.1), channel_id=1, source_target_pairs={{4,0},{8,4},{12,8},{16,12},{20,16},{24,20},{28,24},{5,1},{9,5},{13... | collective-permute-start | bytes 3145736 | tf_op jit(solution)/shard_map/ppermute | solution.py:23
  4.7 1.6 %copy-start.2 = (f32[4,2,256,256]{3,2,1,0:T(8,128)S(1)}, f32[4,2,256,256]{3,2,1,0:T(8,128)}, u32[]{:S(2)}) copy-start(f32[4,2,256,256]{3,2,1,0:T(8,128)} %probe_ref.1) | copy-start | bytes 6291460
  6.3 1.2 %copy-start.3 = (f32[4,256,256]{2,1,0:T(8,128)S(1)}, f32[4,256,256]{2,1,0:T(8,128)}, u32[]{:S(2)}) copy-start(f32[4,256,256]{2,1,0:T(8,128)} %diffraction_ref.1) | copy-start | bytes 3145732
  22.6 13.6 %collective-permute-start.1 = (f32[4,9,8,256]{3,2,1,0:T(8,128)S(1)}, f32[4,9,8,256]{3,2,1,0:T(8,128)S(1)}, u32[]{:S(2)}, u32[]{:S(2)}) collective-permute-start(f32[4,9,8,256]{3,2,1,0:T(8,128)S(1)} %get-tuple-element.71), channel_id=1, source_target_pairs={{0,4},{4,0},{8,12},{12,8},{16,20},{20,16},{24,28},{28,24},{1,5},{5... | collective-permute-start | bytes 884744 | tf_op jit(solution)/shard_map/ppermute | solution.py:575
  36.2 2.4 %collective-permute-start.2 = (f32[3,4,9,8,256]{4,3,2,1,0:T(8,128)S(1)}, f32[3,4,9,8,256]{4,3,2,1,0:T(8,128)S(1)}, u32[]{:S(2)}, u32[]{:S(2)}) collective-permute-start(f32[3,4,9,8,256]{4,3,2,1,0:T(8,128)S(1)} %get-tuple-element.72), channel_id=1, source_target_pairs={{0,4},{4,0},{8,12},{12,8},{16,20},{20,16},{24,28},{28,24},{1,5},{5... | collective-permute-start | bytes 2654216 | tf_op jit(solution)/shard_map/ppermute | solution.py:575
  36.6 6.0 %collective-permute-start.5 = (f32[2,9,8,256]{3,2,1,0:T(8,128)S(1)}, f32[2,9,8,256]{3,2,1,0:T(8,128)S(1)}, u32[]{:S(2)}, u32[]{:S(2)}) collective-permute-start(f32[2,9,8,256]{3,2,1,0:T(8,128)S(1)} %get-tuple-element.104), channel_id=1, source_target_pairs={{0,1},{1,0},{2,3},{3,2},{4,5},{5,4},{6,7},{7,6},{8,9},{9,8},{10,11... | collective-permute-start | bytes 442376 | tf_op jit(solution)/shard_map/ppermute | solution.py:571
  36.7 6.0 %collective-permute-start.3 = (f32[2,9,8,256]{3,2,1,0:T(8,128)S(1)}, f32[2,9,8,256]{3,2,1,0:T(8,128)S(1)}, u32[]{:S(2)}, u32[]{:S(2)}) collective-permute-start(f32[2,9,8,256]{3,2,1,0:T(8,128)S(1)} %get-tuple-element.105), channel_id=1, source_target_pairs={{0,2},{1,3},{2,0},{3,1},{4,6},{5,7},{6,4},{7,5},{8,10},{9,11},{10,... | collective-permute-start | bytes 442376 | tf_op jit(solution)/shard_map/ppermute | solution.py:571
  38.7 26.6 %collective-permute-start.10 = (f32[2048,128]{1,0:T(8,128)S(1)}, f32[2048,128]{1,0:T(8,128)S(1)}, u32[]{:S(2)}, u32[]{:S(2)}) collective-permute-start(f32[2048,128]{1,0:T(8,128)S(1)} %get-tuple-element.82), channel_id=1, source_target_pairs={{0,4},{4,8},{8,12},{12,16},{16,20},{20,24},{24,28},{1,5},{5,9},{9,... | collective-permute-start | bytes 3145736 | tf_op jit(solution)/shard_map/ppermute | solution.py:23
  42.7 8.7 %collective-permute-start.6 = (f32[4,9,8,256]{3,2,1,0:T(8,128)S(1)}, f32[4,9,8,256]{3,2,1,0:T(8,128)S(1)}, u32[]{:S(2)}, u32[]{:S(2)}) collective-permute-start(f32[4,9,8,256]{3,2,1,0:T(8,128)S(1)} %get-tuple-element.100), channel_id=1, source_target_pairs={{0,2},{1,3},{2,0},{3,1},{4,6},{5,7},{6,4},{7,5},{8,10},{9,11},{10,... | collective-permute-start | bytes 884744 | tf_op jit(solution)/shard_map/ppermute | solution.py:571
  43.1 8.3 %collective-permute-start.4 = (f32[4,9,8,256]{3,2,1,0:T(8,128)S(1)}, f32[4,9,8,256]{3,2,1,0:T(8,128)S(1)}, u32[]{:S(2)}, u32[]{:S(2)}) collective-permute-start(f32[4,9,8,256]{3,2,1,0:T(8,128)S(1)} %get-tuple-element.101), channel_id=1, source_target_pairs={{0,1},{1,0},{2,3},{3,2},{4,5},{5,4},{6,7},{7,6},{8,9},{9,8},{10,11... | collective-permute-start | bytes 884744 | tf_op jit(solution)/shard_map/ppermute | solution.py:571
  51.4 9.8 %collective-permute-start.9 = (f32[9,8,256]{2,1,0:T(8,128)S(1)}, f32[9,8,256]{2,1,0:T(8,128)S(1)}, u32[]{:S(2)}, u32[]{:S(2)}) collective-permute-start(f32[9,8,256]{2,1,0:T(8,128)S(1)} %get-tuple-element.96), channel_id=1, source_target_pairs={{0,24},{4,28},{8,0},{12,4},{16,8},{20,12},{24,16},{28,20},{1,25},{... | collective-permute-start | bytes 221192 | tf_op jit(solution)/shard_map/ppermute | solution.py:580
  59.2 5.3 %collective-permute-start.8 = (f32[9,8,256]{2,1,0:T(8,128)S(1)}, f32[9,8,256]{2,1,0:T(8,128)S(1)}, u32[]{:S(2)}, u32[]{:S(2)}) collective-permute-start(f32[9,8,256]{2,1,0:T(8,128)S(1)} %get-tuple-element.97), channel_id=1, source_target_pairs={{0,16},{4,20},{8,24},{12,28},{16,0},{20,4},{24,8},{28,12},{1,17},{... | collective-permute-start | bytes 221192 | tf_op jit(solution)/shard_map/ppermute | solution.py:580
  59.2 6.2 %collective-permute-start.7 = (f32[9,8,256]{2,1,0:T(8,128)S(1)}, f32[9,8,256]{2,1,0:T(8,128)S(1)}, u32[]{:S(2)}, u32[]{:S(2)}) collective-permute-start(f32[9,8,256]{2,1,0:T(8,128)S(1)} %get-tuple-element.98), channel_id=1, source_target_pairs={{0,8},{4,12},{8,16},{12,20},{16,24},{20,28},{24,0},{28,4},{1,9},{5... | collective-permute-start | bytes 221192 | tf_op jit(solution)/shard_map/ppermute | solution.py:580
  65.4 5.0 %collective-permute-start.13 = (f32[8,8,256]{2,1,0:T(8,128)S(1)}, f32[8,8,256]{2,1,0:T(8,128)S(1)}, u32[]{:S(2)}, u32[]{:S(2)}) collective-permute-start(f32[8,8,256]{2,1,0:T(8,128)S(1)} %divided.1), channel_id=1, source_target_pairs={{0,24},{4,28},{8,0},{12,4},{16,8},{20,12},{24,16},{28,20},{1,25},{... | collective-permute-start | bytes 196616 | tf_op jit(solution)/shard_map/ppermute | solution.py:580
  67.0 6.5 %collective-permute-start.12 = (f32[8,8,256]{2,1,0:T(8,128)S(1)}, f32[8,8,256]{2,1,0:T(8,128)S(1)}, u32[]{:S(2)}, u32[]{:S(2)}) collective-permute-start(f32[8,8,256]{2,1,0:T(8,128)S(1)} %divided.1), channel_id=1, source_target_pairs={{0,16},{4,20},{8,24},{12,28},{16,0},{20,4},{24,8},{28,12},{1,17},{... | collective-permute-start | bytes 196616 | tf_op jit(solution)/shard_map/ppermute | solution.py:580
  67.0 6.5 %collective-permute-start.11 = (f32[8,8,256]{2,1,0:T(8,128)S(1)}, f32[8,8,256]{2,1,0:T(8,128)S(1)}, u32[]{:S(2)}, u32[]{:S(2)}) collective-permute-start(f32[8,8,256]{2,1,0:T(8,128)S(1)} %divided.1), channel_id=1, source_target_pairs={{0,8},{4,12},{8,16},{12,20},{16,24},{20,28},{24,0},{28,4},{1,9},{5... | collective-permute-start | bytes 196616 | tf_op jit(solution)/shard_map/ppermute | solution.py:580
  73.5 6.4 %collective-permute-start.16 = (f32[4,8,8,256]{3,2,1,0:T(8,128)S(1)}, f32[4,8,8,256]{3,2,1,0:T(8,128)S(1)}, u32[]{:S(2)}, u32[]{:S(2)}) collective-permute-start(f32[4,8,8,256]{3,2,1,0:T(8,128)S(1)} %pad_maximum_fusion.refs_0_), channel_id=1, source_target_pairs={{0,2},{1,3},{2,0},{3,1},{4,6},{5,7},{6,4},{7,5},{8,10},{9,11},{10,... | collective-permute-start | bytes 786440 | tf_op jit(solution)/shard_map/ppermute | solution.py:571
  74.6 6.4 %collective-permute-start.14 = (f32[4,8,8,256]{3,2,1,0:T(8,128)S(1)}, f32[4,8,8,256]{3,2,1,0:T(8,128)S(1)}, u32[]{:S(2)}, u32[]{:S(2)}) collective-permute-start(f32[4,8,8,256]{3,2,1,0:T(8,128)S(1)} %pad_maximum_fusion.refs_0_), channel_id=1, source_target_pairs={{0,1},{1,0},{2,3},{3,2},{4,5},{5,4},{6,7},{7,6},{8,9},{9,8},{10,11... | collective-permute-start | bytes 786440 | tf_op jit(solution)/shard_map/ppermute | solution.py:571
  75.6 8.1 %collective-permute-start.18 = (f32[4,8,8,256]{3,2,1,0:T(8,128)S(1)}, f32[4,8,8,256]{3,2,1,0:T(8,128)S(1)}, u32[]{:S(2)}, u32[]{:S(2)}) collective-permute-start(f32[4,8,8,256]{3,2,1,0:T(8,128)S(1)} %pad_maximum_fusion.refs_0_), channel_id=1, source_target_pairs={{0,4},{4,0},{8,12},{12,8},{16,20},{20,16},{24,28},{28,24},{1,5},{5... | collective-permute-start | bytes 786440 | tf_op jit(solution)/shard_map/ppermute | solution.py:575
  80.0 3.7 %collective-permute-start.20 = (f32[4,8,8,256]{3,2,1,0:T(8,128)S(1)}, f32[4,8,8,256]{3,2,1,0:T(8,128)S(1)}, u32[]{:S(2)}, u32[]{:S(2)}) collective-permute-start(f32[4,8,8,256]{3,2,1,0:T(8,128)S(1)} %collective-permute-done.16.refs_2_), channel_id=1, source_target_pairs={{0,4},{4,0},{8,12},{12,8},{16,20},{20,16},{24,28},{28,24},{1,5},{5... | collective-permute-start | bytes 786440 | tf_op jit(solution)/shard_map/ppermute | solution.py:575
  81.0 2.7 %collective-permute-start.19 = (f32[4,8,8,256]{3,2,1,0:T(8,128)S(1)}, f32[4,8,8,256]{3,2,1,0:T(8,128)S(1)}, u32[]{:S(2)}, u32[]{:S(2)}) collective-permute-start(f32[4,8,8,256]{3,2,1,0:T(8,128)S(1)} %collective-permute-done.14.refs_1_), channel_id=1, source_target_pairs={{0,4},{4,0},{8,12},{12,8},{16,20},{20,16},{24,28},{28,24},{1,5},{5... | collective-permute-start | bytes 786440 | tf_op jit(solution)/shard_map/ppermute | solution.py:575
  81.0 6.0 %collective-permute-start.17 = (f32[2,8,8,256]{3,2,1,0:T(8,128)S(1)}, f32[2,8,8,256]{3,2,1,0:T(8,128)S(1)}, u32[]{:S(2)}, u32[]{:S(2)}) collective-permute-start(f32[2,8,8,256]{3,2,1,0:T(8,128)S(1)} %slice.153), channel_id=1, source_target_pairs={{0,1},{1,0},{2,3},{3,2},{4,5},{5,4},{6,7},{7,6},{8,9},{9,8},{10,11... | collective-permute-start | bytes 393224 | tf_op jit(solution)/shard_map/ppermute | solution.py:571
  82.1 5.7 %collective-permute-start.15 = (f32[2,8,8,256]{3,2,1,0:T(8,128)S(1)}, f32[2,8,8,256]{3,2,1,0:T(8,128)S(1)}, u32[]{:S(2)}, u32[]{:S(2)}) collective-permute-start(f32[2,8,8,256]{3,2,1,0:T(8,128)S(1)} %slice.152), channel_id=1, source_target_pairs={{0,2},{1,3},{2,0},{3,1},{4,6},{5,7},{6,4},{7,5},{8,10},{9,11},{10,... | collective-permute-start | bytes 393224 | tf_op jit(solution)/shard_map/ppermute | solution.py:571
  87.8 1.3 %collective-permute-start.21 = (f32[2,8,8,256]{3,2,1,0:T(8,128)S(1)}, f32[2,8,8,256]{3,2,1,0:T(8,128)S(1)}, u32[]{:S(2)}, u32[]{:S(2)}) collective-permute-start(f32[2,8,8,256]{3,2,1,0:T(8,128)S(1)} %collective-permute-done.15.refs_0_), channel_id=1, source_target_pairs={{0,4},{4,0},{8,12},{12,8},{16,20},{20,16},{24,28},{28,24},{1,5},{5... | collective-permute-start | bytes 393224 | tf_op jit(solution)/shard_map/ppermute | solution.py:575
  87.8 1.5 %collective-permute-start.22 = (f32[2,8,8,256]{3,2,1,0:T(8,128)S(1)}, f32[2,8,8,256]{3,2,1,0:T(8,128)S(1)}, u32[]{:S(2)}, u32[]{:S(2)}) collective-permute-start(f32[2,8,8,256]{3,2,1,0:T(8,128)S(1)} %collective-permute-done.17.refs_1_), channel_id=1, source_target_pairs={{0,4},{4,0},{8,12},{12,8},{16,20},{20,16},{24,28},{28,24},{1,5},{5... | collective-permute-start | bytes 393224 | tf_op jit(solution)/shard_map/ppermute | solution.py:575

commit v2 on v0

--- a/solution.py
+++ b/solution.py
@@ -41,7 +41,24 @@
     for odd in range(2):
         angle = 2.0 * math.pi * ((n * (2 * q + odd)) % side) / side
         made += [np.cos(angle) / math.sqrt(side), -np.sin(angle) / math.sqrt(side)]
+    quarter = side // 4
+    q, n = np.arange(quarter)[:, None], np.arange(quarter)[None, :]
+    for rest in range(4):
+        angle = 2.0 * math.pi * ((n * (4 * q + rest)) % side) / side
+        re, im = np.cos(angle) / math.sqrt(side), -np.sin(angle) / math.sqrt(side)
+        made.append(np.block([[re, -im], [im, re]]))
     return np.stack(made).astype(np.float32)
+
+
+def fill_rows_table(factor_ref, rows_table_ref):
+    half = factor_ref.shape[1]
+    left, right = pl.ds(0, half), pl.ds(half, half)
+    for rest in range(4):
+        for turned in range(2):
+            exact = factor_ref[4 + rest]
+            for rows, term in zip((left, right), split(exact.T if turned else exact)):
+                rows_table_ref[4 * turned + rest, rows, left] = term
+                rows_table_ref[4 * turned + rest, rows, right] = term
 
 
 def fill_table(factor_ref, table_ref):
@@ -60,17 +77,19 @@
                 table_ref[term, entry, right, right] = re
 
 
-def parity_order(side):
-    half = side // 2
+def orders(side):
+    half, quarter = side // 2, side // 4
     first = lax.broadcasted_iota(jnp.int32, (side, side), 0)
     second = lax.broadcasted_iota(jnp.int32, (side, side), 1)
 
-    def moves(source, place):
-        odd = (place >= half).astype(jnp.int32)
-        hit = source == 2 * (place - odd * half) + odd
+    def moves(hit):
         return hit.astype(jnp.float32).astype(jnp.bfloat16)
 
-    return moves(first, second), moves(second, first)
+    odd = second // half
+    rest = first // quarter
+    by_lanes = moves(first == 2 * (second - odd * half) + odd)
+    by_rows = moves(second == 4 * (first - rest * quarter) + rest)
+    return by_lanes, by_rows
 
 
 def split(x):
@@ -95,16 +114,16 @@
         )
 
 
-def transform_rows(terms, rows, table_ref, table, out):
-    side = out.shape[2]
-    for half in range(2):
-        high = terms[half, rows, pl.ds(0, side)]
-        low = terms[half, rows, pl.ds(side, side)]
-        t_high, t_low = table_ref[0, table + half], table_ref[1, table + half]
-        out[half, rows, :] = dot(
-            jnp.concatenate([t_high, t_high, t_low], axis=1),
-            jnp.concatenate([high, low, high], axis=0),
-        )
+def transform_rows(columns, rows, rows_table_ref, table, wide):
+    for rest in range(4):
+        wide[rest, rows, :] = dot(rows_table_ref[table + rest], columns[rest, rows, :])
+
+
+def keep_rows(columns, rest, base, start, real, imag):
+    quarter = columns.shape[2] // 4
+    for part, value in enumerate((real, imag)):
+        for term, piece in enumerate(split(value)):
+            columns[rest, pl.ds(base + (2 * term + part) * quarter + start, value.shape[0]), :] = piece
 
 
 def keep(terms, half, start, value):
@@ -126,6 +145,7 @@
     count_ref,
     probe_ref,
     table_ref,
+    rows_table_ref,
     extended,
     gradient,
     sums,
@@ -134,6 +154,8 @@
     window,
     terms,
     result,
+    columns,
+    wide,
     back,
 ):
     modes, _, side, _ = probe_ref.shape
@@ -179,44 +201,59 @@
                     keep(terms, 0, start, beside(real[0] + real[1], imag[0] + imag[1]))
                     keep(terms, 1, start, beside(real[0] - real[1], imag[0] - imag[1]))
             transform(terms, rows_of(stream), table_ref, 0, result)
-        halves = [pl.ds(start, ROWS) for start in range(0, half, ROWS)]
+        quarter = side // 4
+        quarters = range(0, quarter, ROWS // 2)
+
+        def taken(rest, base, part, start):
+            at = base + part * quarter + start
+            return wide[rest, pl.ds(at, ROWS // 2), :] + wide[rest, pl.ds(at + half, ROWS // 2), :]
+
         for mode in range(modes):
             base = mode * side
-            for rows in halves:
-                for part, side_ in enumerate((left, right)):
-                    top, bottom = pl.ds(base + rows.start, ROWS), pl.ds(base + half + rows.start, ROWS)
-                    above = beside(result[0, top, side_], result[1, top, side_])
-                    below = beside(result[0, bottom, side_], result[1, bottom, side_])
-                    start = base + part * half + rows.start
-                    keep(terms, 0, start, above + below)
-                    keep(terms, 1, start, above - below)
-            transform_rows(terms, pl.ds(base, side), table_ref, 2, result)
-        for odd in range(2):
-            for rows in halves:
-                far = [
-                    [result[odd, pl.ds(mode * side + part * half + rows.start, ROWS), :] for part in range(2)]
-                    for mode in range(modes)
+            for start in quarters:
+                x = [
+                    [
+                        beside(*[result[odd, pl.ds(base + j * quarter + start, ROWS // 2), side_] for odd in range(2)])
+                        for side_ in (left, right)
+                    ]
+                    for j in range(4)
                 ]
-                intensity = jnp.zeros((ROWS, side), jnp.float32)
+                s0, d0 = [x[0][p] + x[2][p] for p in range(2)], [x[0][p] - x[2][p] for p in range(2)]
+                s1, d1 = [x[1][p] + x[3][p] for p in range(2)], [x[1][p] - x[3][p] for p in range(2)]
+                keep_rows(columns, 0, base, start, s0[0] + s1[0], s0[1] + s1[1])
+                keep_rows(columns, 1, base, start, d0[0] + d1[1], d0[1] - d1[0])
+                keep_rows(columns, 2, base, start, s0[0] - s1[0], s0[1] - s1[1])
+                keep_rows(columns, 3, base, start, d0[0] - d1[1], d0[1] + d1[0])
+            transform_rows(columns, pl.ds(base, side), rows_table_ref, 0, wide)
+        for rest in range(4):
+            for start in quarters:
+                far = [[taken(rest, mode * side, part, start) for part in range(2)] for mode in range(modes)]
+                intensity = jnp.zeros((ROWS // 2, side), jnp.float32)
                 for real, imag in far:
                     intensity = intensity + real * real + imag * imag
-                amount = measured[index, pl.ds(odd * half + rows.start, ROWS), :]
+                amount = measured[index, pl.ds(rest * quarter + start, ROWS // 2), :]
                 ratio = amount * lax.rsqrt(amount * jnp.maximum(intensity, 1.0))
-                for mode in range(modes):
-                    for part in range(2):
-                        keep(terms, odd, mode * side + part * half + rows.start, far[mode][part] * ratio)
+                for mode, (real, imag) in enumerate(far):
+                    keep_rows(columns, rest, mode * side, start, real * ratio, imag * ratio)
         for mode in range(modes):
-            transform_rows(terms, pl.ds(mode * side, side), table_ref, 0, result)
+            transform_rows(columns, pl.ds(mode * side, side), rows_table_ref, 4, wide)
         for stream in streams:
             for mode in stream:
                 base = mode * side
-                for rows in halves:
-                    real, imag = pl.ds(base + rows.start, ROWS), pl.ds(base + half + rows.start, ROWS)
-                    for odd, side_ in enumerate((left, right)):
-                        a = beside(result[0, real, side_], result[0, imag, side_])
-                        b = beside(result[1, real, side_], result[1, imag, side_])
-                        keep(terms, odd, base + rows.start, a + b)
-                        keep(terms, odd, base + half + rows.start, a - b)
+                for start in quarters:
+                    z = [[taken(rest, base, part, start) for part in range(2)] for rest in range(4)]
+                    s0, d0 = [z[0][p] + z[2][p] for p in range(2)], [z[0][p] - z[2][p] for p in range(2)]
+                    s1, d1 = [z[1][p] + z[3][p] for p in range(2)], [z[1][p] - z[3][p] for p in range(2)]
+                    x = [
+                        [s0[0] + s1[0], s0[1] + s1[1]],
+                        [d0[0] - d1[1], d0[1] + d1[0]],
+                        [s0[0] - s1[0], s0[1] - s1[1]],
+                        [d0[0] + d1[1], d0[1] - d1[0]],
+                    ]
+                    for j, (real, imag) in enumerate(x):
+                        at = base + j * quarter + start
+                        keep(terms, 0, at, beside(real[:, :half], imag[:, :half]))
+                        keep(terms, 1, at, beside(real[:, half:], imag[:, half:]))
             transform(terms, rows_of(stream), table_ref, 2, result)
         for number, stream in enumerate(streams):
             for rows in pieces:
@@ -280,10 +317,13 @@
     power,
     probe_out,
     table_out,
+    rows_table_out,
     scale_out,
     window,
     terms,
     result,
+    columns,
+    wide,
     back,
     semaphore,
 ):
@@ -299,7 +339,8 @@
     scale_out[...] = jnp.full(scale_out.shape, 1.0 / jnp.max(total))
     probe_out[...] = probe_ref[...]
     fill_table(factor_ref, table_out)
-    by_lanes, by_rows = parity_order(side)
+    by_lanes, by_rows = orders(side)
+    fill_rows_table(factor_ref, rows_table_out)
 
     def order(index, carry):
         high, low = split(diffraction_ref[index])
@@ -312,8 +353,8 @@
     lax.fori_loop(0, count_ref[0, 0], order, 0)
     copy.wait()
     all_slots(
-        True, tile_out.shape[0] // SUBLANES, place_ref, count_ref, probe_ref, table_out, tile_out,
-        gradient, sums, power, measured, window, terms, result, back,
+        True, tile_out.shape[0] // SUBLANES, place_ref, count_ref, probe_ref, table_out, rows_table_out, tile_out,
+        gradient, sums, power, measured, window, terms, result, columns, wide, back,
     )
 
 
@@ -329,6 +370,7 @@
     power,
     probe_ref,
     table_ref,
+    rows_table_ref,
     gradient,
     spill_out,
     mine_out,
@@ -340,6 +382,8 @@
     window,
     terms,
     result,
+    columns,
+    wide,
     back,
 ):
     modes = probe_ref.shape[0]
@@ -350,8 +394,8 @@
     gradient[pl.ds(tile_rows, halo_rows), :] = jnp.zeros((halo_rows, LANES), jnp.float32)
     sums[...] = sums_ref[...]
     all_slots(
-        False, tile_rows // SUBLANES, place_ref, count_ref, probe_ref, table_ref, extended,
-        gradient, sums, power, measured, window, terms, result, back,
+        False, tile_rows // SUBLANES, place_ref, count_ref, probe_ref, table_ref, rows_table_ref, extended,
+        gradient, sums, power, measured, window, terms, result, columns, wide, back,
     )
     spill_out[...] = gradient[pl.ds(tile_rows, halo_rows), :]
     core, group, layer = here_ref[0, 0], here_ref[0, 1], here_ref[0, 2]
@@ -383,6 +427,8 @@
         pltpu.VMEM((2, side, side), f32),
         pltpu.VMEM((2, modes * side, 2 * side), jnp.bfloat16),
         pltpu.VMEM((2, modes * side, side), f32),
+        pltpu.VMEM((4, modes * side, side), jnp.bfloat16),
+        pltpu.VMEM((4, modes * side, side), f32),
         pltpu.VMEM((2, side, side), f32),
     ]
     shape = jax.ShapeDtypeStruct
@@ -397,12 +443,13 @@
             shape((side, side), f32),
             shape(probe.shape, f32),
             shape((2, 4, side, side), jnp.bfloat16),
+            shape((8, side, side), jnp.bfloat16),
             shape((1, LANES), f32),
         ),
         in_specs=[smem, smem, pl.BlockSpec(memory_space=pl.ANY), vmem, vmem, vmem],
-        out_specs=(vmem,) * 8,
+        out_specs=(vmem,) * 9,
         scratch_shapes=work + [pltpu.SemaphoreType.DMA],
-        compiler_params=pltpu.CompilerParams(vmem_limit_bytes=28 * 1024 * 1024),
+        compiler_params=pltpu.CompilerParams(vmem_limit_bytes=32 * 1024 * 1024),
         cost_estimate=cost,
         name="slots_inside",
     )(place, count, tile, probe, diffraction, jnp.asarray(tables(side)))
@@ -416,14 +463,14 @@
             shape((layers, *chunk), f32),
             shape((planes - 1, SUBLANES, side), f32),
         ),
-        in_specs=[smem, smem, smem] + [vmem] * 8,
+        in_specs=[smem, smem, smem] + [vmem] * 9,
         out_specs=(vmem,) * 6,
         scratch_shapes=[
             pltpu.VMEM((tile.shape[0] + halo.shape[0], LANES), f32),
             pltpu.VMEM((chunks, *chunk), f32),
         ]
         + work,
-        compiler_params=pltpu.CompilerParams(vmem_limit_bytes=30 * 1024 * 1024),
+        compiler_params=pltpu.CompilerParams(vmem_limit_bytes=34 * 1024 * 1024),
         cost_estimate=cost,
         name="slots_across",
     )(place, count, here, halo, *begun)

time: 92.3 us -> 90.4 us (0.979)
  Pallas kernels: 32.2 us -> 30.2 us
  starting transfers between devices: 24.2 us -> 22.9 us
  local copies, waits for them, and re-layouts: 4.59 us -> 5.63 us
    ppermute x6, starting transfers between devices: 12.4 us -> 7.16 us  [up_layers(): lax.ppermute(block, 'region', [(i, (i + 2 * step) % regions) for i in ran...]
    ppermute x8, starting transfers between devices: 7.39 us -> 11.5 us  [across(): lax.ppermute(block, 'group', [(i, i ^ hop) for i in range(lax.axis_size('...]
    ppermute x8, waiting for transfers between devices: 12.8 us -> 15.7 us  [across(): lax.ppermute(block, 'group', [(i, i ^ hop) for i in range(lax.axis_size('...]
    ppermute x7, waiting for transfers between devices: 4.66 us -> 2.6 us  [from_partner(): lax.ppermute(block, 'region', [(i, i ^ 1) for i in range(lax.axis_size('r...]
    unnamed x13, local copies, waits for them, and re-layouts: 4.51 us -> 5.55 us
    pallas_call x1, Pallas kernels: 12.5 us -> 11.5 us  [gradient_step(): pl.pallas_call(second_kernel, out_shape=(shape((tile.shape[0] + halo.shap...]
    pallas_call x1, Pallas kernels: 13.9 us -> 12.9 us  [gradient_step(): pl.pallas_call(first_kernel, out_shape=(shape(tile.shape, f32), shape(til...]
  transfers between devices with their start and end apart: 23 -> 23, of which waited for: 18 -> 14; matrix products, arithmetic and copies ran while one was open for 1% -> 1% of each run, Pallas kernels for 20% -> 19%
where the time goes in v2:
time: 90.4 us; the launch traced here: 88.7 us
  Pallas kernels  30.2 us (33%)
  waiting for transfers between devices  27.9 us (31%)
  starting transfers between devices  22.9 us (25%)
  local copies, waits for them, and re-layouts  5.63 us (6%)
  between operations  1.65 us (2%)
    ppermute x8, waiting for transfers between devices, across(): lax.ppermute(block, 'group', [(i, i ^ hop) for i in range(lax.axis_size('...  15.7 us
    pallas_call x1, Pallas kernels, gradient_step(): pl.pallas_call(first_kernel, out_shape=(shape(tile.shape, f32), shape(til...  12.9 us
    ppermute x8, starting transfers between devices, across(): lax.ppermute(block, 'group', [(i, i ^ hop) for i in range(lax.axis_size('...  11.5 us
    pallas_call x1, Pallas kernels, gradient_step(): pl.pallas_call(second_kernel, out_shape=(shape((tile.shape[0] + halo.shap...  11.5 us
    ppermute x6, waiting for transfers between devices, up_layers(): lax.ppermute(block, 'region', [(i, (i + 2 * step) % regions) for i in ran...  9.57 us
    ppermute x6, starting transfers between devices, up_layers(): lax.ppermute(block, 'region', [(i, (i + 2 * step) % regions) for i in ran...  7.16 us
    unnamed x13, local copies, waits for them, and re-layouts  5.55 us
    ppermute x2, starting transfers between devices, shifted(): return lax.ppermute(block, axis, route)  3.43 us
  transfers between devices with their start and end apart: 23, of which 14 were waited for; matrix products, arithmetic and copies ran while one was open for 1% of the time, Pallas kernels for 19%

profile of v2, /device:TPU:0, one launch (start us, length us, event | category | flops | bytes accessed | tf_op | source)
XLA Modules:
  0.0 88.7 jit_solution(14582909011436142314)
XLA Ops:
  0.6 0.0 copy-start.5
  0.6 1.6 %copy-done = f32[512,2,512]{2,1,0:T(2,128)S(1)} copy-done((f32[512,2,512]{2,1,0:T(2,128)S(1)}, f32[512,2,512]{2,1,0:T(2,128)}, u32[]{:S(2)}) %copy-start) | copy-done | bytes 2097176
  2.2 0.1 first_rows.1
  2.3 1.4 %collective-permute-start = (f32[2048,128]{1,0:T(8,128)S(1)}, f32[2048,128]{1,0:T(8,128)}, u32[]{:S(2)}, u32[]{:S(2)}) collective-permute-start(f32[2048,128]{1,0:T(8,128)S(1)} %first_rows.1), channel_id=1, source_target_pairs={{4,0},{8,4},{12,8},{16,12},{20,16},{24,20},{28,24},{5,1},{9,5},{13... | collective-permute-start | bytes 3145736 | tf_op jit(solution)/shard_map/ppermute | solution.py:22
  4.4 0.1 copy.10
  4.5 0.1 pad_add_fusion
  4.6 0.1 add_bitcast_fusion.here_ref
  4.7 0.0 copy-done.1
  4.7 1.6 %copy-done.2 = f32[4,2,256,256]{3,2,1,0:T(8,128)S(1)} copy-done((f32[4,2,256,256]{3,2,1,0:T(8,128)S(1)}, f32[4,2,256,256]{3,2,1,0:T(8,128)}, u32[]{:S(2)}) %copy-start.2) | copy-done | bytes 2097176
  6.3 1.2 %copy-done.3 = f32[4,256,256]{2,1,0:T(8,128)S(1)} copy-done((f32[4,256,256]{2,1,0:T(8,128)S(1)}, f32[4,256,256]{2,1,0:T(8,128)}, u32[]{:S(2)}) %copy-start.3) | copy-done | bytes 1048600
  7.5 1.0 %copy-done.4 = f32[8,128,128]{2,1,0:T(8,128)S(1)} copy-done((f32[8,128,128]{2,1,0:T(8,128)S(1)}, f32[8,128,128]{2,1,0:T(8,128)}, u32[]{:S(2)}) %copy-start.4) | copy-done | bytes 524312
  8.5 12.9 %slots_inside.1 = (f32[4096,128]{1,0:T(8,128)S(1)}, f32[4096,128]{1,0:T(8,128)S(1)}, f32[32,9,8,256]{3,2,1,0:T(8,128)S(1)}, f32[4,256,256]{2,1,0:T(8,128)S(1)}, ...) custom-call(s32[4,2]{1,0:T(4,128)S(1)} %broadcast_subtract_fusion.pl, ...), custom_call_target="tpu_custom_call" | custom-call | flops 12884901888 | bytes 16777216 | tf_op jit(solution)/shard_map/slots_inside/pallas_call | solution.py:436
  21.4 0.0 collective-permute-done.halo_ref
  21.4 11.5 %slots_across.1 = (f32[6144,128]{1,0:T(8,128)S(1)}, f32[2048,128]{1,0:T(8,128)S(1)}, f32[4,4,9,8,256]{4,3,2,1,0:T(8,128)S(1)}, f32[3,4,9,8,256]{4,3,2,1,0:T(8,12...) custom-call(s32[4,2]{1,0:T(4,128)S(1)} %broadcast_subtract_fusion.place_ref, s32[1,1]{1,0:T(1,128)S(6)} %copy.17.count_ref, ...), custom_call_target="tpu_custom_call" | custom-call | flops 12884901888 | bytes 16777216 | tf_op jit(solution)/shard_map/slots_across/pallas_call | solution.py:456
  32.9 0.1 collective-permute-start.1
  33.0 1.6 %collective-permute-done.1 = f32[4,9,8,256]{3,2,1,0:T(8,128)S(1)} collective-permute-done((f32[4,9,8,256]{3,2,1,0:T(8,128)S(1)}, f32[4,9,8,256]{3,2,1,0:T(8,128)S(1)}, u32[]{:S(2)}, u32[]{:S(2)}) %collective-permute-start.1) | collective-permute-done | bytes 294944 | tf_op jit(solution)/shard_map/ppermute | solution.py:605
  34.6 0.1 collective-permute-start.2
  34.8 0.1 collective-permute-start.5
  34.8 4.0 %collective-permute-start.3 = (f32[2,9,8,256]{3,2,1,0:T(8,128)S(1)}, f32[2,9,8,256]{3,2,1,0:T(8,128)S(1)}, u32[]{:S(2)}, u32[]{:S(2)}) collective-permute-start(f32[2,9,8,256]{3,2,1,0:T(8,128)S(1)} %get-tuple-element.107), channel_id=1, source_target_pairs={{0,2},{1,3},{2,0},{3,1},{4,6},{5,7},{6,4},{7,5},{8,10},{9,11},{10,... | collective-permute-start | bytes 442376 | tf_op jit(solution)/shard_map/ppermute | solution.py:601
  38.9 0.0 collective-permute-done.2
  38.9 0.1 slice_add_fusion
  39.0 2.0 %collective-permute-start.10 = (f32[2048,128]{1,0:T(8,128)S(1)}, f32[2048,128]{1,0:T(8,128)S(1)}, u32[]{:S(2)}, u32[]{:S(2)}) collective-permute-start(f32[2048,128]{1,0:T(8,128)S(1)} %get-tuple-element.84), channel_id=1, source_target_pairs={{0,4},{4,8},{8,12},{12,16},{16,20},{20,24},{24,28},{1,5},{5,9},{9,... | collective-permute-start | bytes 3145736 | tf_op jit(solution)/shard_map/ppermute | solution.py:22
  41.0 0.0 collective-permute-done.5
  41.1 2.0 %collective-permute-done.3 = f32[2,9,8,256]{3,2,1,0:T(8,128)S(1)} collective-permute-done((f32[2,9,8,256]{3,2,1,0:T(8,128)S(1)}, f32[2,9,8,256]{3,2,1,0:T(8,128)S(1)}, u32[]{:S(2)}, u32[]{:S(2)}) %collective-permute-start.3) | collective-permute-done | bytes 147488 | tf_op jit(solution)/shard_map/ppermute | solution.py:601
  43.1 1.8 %collective-permute-start.6 = (f32[4,9,8,256]{3,2,1,0:T(8,128)S(1)}, f32[4,9,8,256]{3,2,1,0:T(8,128)S(1)}, u32[]{:S(2)}, u32[]{:S(2)}) collective-permute-start(f32[4,9,8,256]{3,2,1,0:T(8,128)S(1)} %get-tuple-element.102), channel_id=1, source_target_pairs={{0,2},{1,3},{2,0},{3,1},{4,6},{5,7},{6,4},{7,5},{8,10},{9,11},{10,... | collective-permute-start | bytes 884744 | tf_op jit(solution)/shard_map/ppermute | solution.py:601
  44.9 1.7 %collective-permute-start.4 = (f32[4,9,8,256]{3,2,1,0:T(8,128)S(1)}, f32[4,9,8,256]{3,2,1,0:T(8,128)S(1)}, u32[]{:S(2)}, u32[]{:S(2)}) collective-permute-start(f32[4,9,8,256]{3,2,1,0:T(8,128)S(1)} %get-tuple-element.103), channel_id=1, source_target_pairs={{0,1},{1,0},{2,3},{3,2},{4,5},{5,4},{6,7},{7,6},{8,9},{9,8},{10,11... | collective-permute-start | bytes 884744 | tf_op jit(solution)/shard_map/ppermute | solution.py:601
  46.5 1.4 %written.1 = (f32[4096,128]{1,0:T(8,128)}, f32[2048,128]{1,0:T(8,128)S(1)}) custom-call(f32[4096,128]{1,0:T(8,128)S(1)} %get-tuple-element.62.tile_ref, f32[6144,128]{1,0:T(8,128)S(1)} %get-tuple-element.78.gradient_ref, f32[1,128]{1,0:T(1,128)S(1)} %get-tuple-element.79.scale_ref), custom_call_target="tpu_custom_call" | custom-call | bytes 4194304 | tf_op jit(solution)/shard_map/written/pallas_call | solution.py:497
  48.0 4.7 %collective-permute-done.6 = f32[4,9,8,256]{3,2,1,0:T(8,128)S(1)} collective-permute-done((f32[4,9,8,256]{3,2,1,0:T(8,128)S(1)}, f32[4,9,8,256]{3,2,1,0:T(8,128)S(1)}, u32[]{:S(2)}, u32[]{:S(2)}) %collective-permute-start.6) | collective-permute-done | bytes 294944 | tf_op jit(solution)/shard_map/ppermute | solution.py:601
  52.7 0.7 collective-permute-done.4
  53.4 0.1 fusion.5
  53.4 3.3 %collective-permute-start.9 = (f32[9,8,256]{2,1,0:T(8,128)S(1)}, f32[9,8,256]{2,1,0:T(8,128)S(1)}, u32[]{:S(2)}, u32[]{:S(2)}) collective-permute-start(f32[9,8,256]{2,1,0:T(8,128)S(1)} %get-tuple-element.98), channel_id=1, source_target_pairs={{0,24},{4,28},{8,0},{12,4},{16,8},{20,12},{24,16},{28,20},{1,25},{... | collective-permute-start | bytes 221192 | tf_op jit(solution)/shard_map/ppermute | solution.py:610
  56.7 0.0 collective-permute-start.8
  56.8 0.7 collective-permute-start.7
  57.4 1.4 %collective-permute-done.9.refs_3_ = f32[9,8,256]{2,1,0:T(8,128)S(1)} collective-permute-done((f32[9,8,256]{2,1,0:T(8,128)S(1)}, f32[9,8,256]{2,1,0:T(8,128)S(1)}, u32[]{:S(2)}, u32[]{:S(2)}) %collective-permute-start.9) | collective-permute-done | bytes 73760 | tf_op jit(solution)/shard_map/ppermute | solution.py:610
  58.8 4.7 %collective-permute-done.8.refs_2_ = f32[9,8,256]{2,1,0:T(8,128)S(1)} collective-permute-done((f32[9,8,256]{2,1,0:T(8,128)S(1)}, f32[9,8,256]{2,1,0:T(8,128)S(1)}, u32[]{:S(2)}, u32[]{:S(2)}) %collective-permute-start.8) | collective-permute-done | bytes 73760 | tf_op jit(solution)/shard_map/ppermute | solution.py:610
  63.4 0.0 collective-permute-done.7.refs_1_
  63.4 0.0 collective-permute-done.10.arrived_ref
  63.5 1.3 %collective-permute-start.13 = (f32[8,8,256]{2,1,0:T(8,128)S(1)}, f32[8,8,256]{2,1,0:T(8,128)S(1)}, u32[]{:S(2)}, u32[]{:S(2)}) collective-permute-start(f32[8,8,256]{2,1,0:T(8,128)S(1)} %divided.1), channel_id=1, source_target_pairs={{0,24},{4,28},{8,0},{12,4},{16,8},{20,12},{24,16},{28,20},{1,25},{... | collective-permute-start | bytes 196616 | tf_op jit(solution)/shard_map/ppermute | solution.py:610
  64.7 0.0 collective-permute-start.12
  64.7 1.9 %collective-permute-start.11 = (f32[8,8,256]{2,1,0:T(8,128)S(1)}, f32[8,8,256]{2,1,0:T(8,128)S(1)}, u32[]{:S(2)}, u32[]{:S(2)}) collective-permute-start(f32[8,8,256]{2,1,0:T(8,128)S(1)} %divided.1), channel_id=1, source_target_pairs={{0,8},{4,12},{8,16},{12,20},{16,24},{20,28},{24,0},{28,4},{1,9},{5... | collective-permute-start | bytes 196616 | tf_op jit(solution)/shard_map/ppermute | solution.py:610
  66.7 1.1 %with_top.1 = f32[4096,128]{1,0:T(8,128)} custom-call(f32[4096,128]{1,0:T(8,128)} %get-tuple-element.88.held_ref, f32[2048,128]{1,0:T(8,128)S(1)} %get-tuple-element.89.top_ref, f32[2048,128]{1,0:T(8,128)S(1)} %collective-permute-done.10.arrived_ref, f32[1,128]{1,0:T(1,128)S(1)} %get-tuple-element.79.scale_ref), custom_call_target="tpu_custom_call", output_to_operand_aliasing={{}: (0, {})} | custom-call | bytes 2097152 | tf_op jit(solution)/shard_map/with_top/pallas_call | solution.py:587
  67.7 0.1 collective-permute-done.13
  67.8 3.5 %collective-permute-done.12 = f32[8,8,256]{2,1,0:T(8,128)S(1)} collective-permute-done((f32[8,8,256]{2,1,0:T(8,128)S(1)}, f32[8,8,256]{2,1,0:T(8,128)S(1)}, u32[]{:S(2)}, u32[]{:S(2)}) %collective-permute-start.12) | collective-permute-done | bytes 65568 | tf_op jit(solution)/shard_map/ppermute | solution.py:610
  71.3 0.0 collective-permute-done.11
  71.3 1.4 %collective-permute-start.16 = (f32[4,8,8,256]{3,2,1,0:T(8,128)S(1)}, f32[4,8,8,256]{3,2,1,0:T(8,128)S(1)}, u32[]{:S(2)}, u32[]{:S(2)}) collective-permute-start(f32[4,8,8,256]{3,2,1,0:T(8,128)S(1)} %pad_maximum_fusion.refs_0_), channel_id=1, source_target_pairs={{0,2},{1,3},{2,0},{3,1},{4,6},{5,7},{6,4},{7,5},{8,10},{9,11},{10,... | collective-permute-start | bytes 786440 | tf_op jit(solution)/shard_map/ppermute | solution.py:601
  72.8 0.6 collective-permute-start.14
  73.4 0.0 collective-permute-start.18
  73.4 4.4 %collective-permute-done.16.refs_2_ = f32[4,8,8,256]{3,2,1,0:T(8,128)S(1)} collective-permute-done((f32[4,8,8,256]{3,2,1,0:T(8,128)S(1)}, f32[4,8,8,256]{3,2,1,0:T(8,128)S(1)}, u32[]{:S(2)}, u32[]{:S(2)}) %collective-permute-start.16) | collective-permute-done | bytes 262176 | tf_op jit(solution)/shard_map/ppermute | solution.py:601
  77.8 0.0 collective-permute-start.20
  77.8 1.4 %collective-permute-done.14.refs_1_ = f32[4,8,8,256]{3,2,1,0:T(8,128)S(1)} collective-permute-done((f32[4,8,8,256]{3,2,1,0:T(8,128)S(1)}, f32[4,8,8,256]{3,2,1,0:T(8,128)S(1)}, u32[]{:S(2)}, u32[]{:S(2)}) %collective-permute-start.14) | collective-permute-done | bytes 262176 | tf_op jit(solution)/shard_map/ppermute | solution.py:601
  79.1 0.0 collective-permute-start.19
  79.2 0.7 collective-permute-start.17
  79.9 1.2 %collective-permute-start.15 = (f32[2,8,8,256]{3,2,1,0:T(8,128)S(1)}, f32[2,8,8,256]{3,2,1,0:T(8,128)S(1)}, u32[]{:S(2)}, u32[]{:S(2)}) collective-permute-start(f32[2,8,8,256]{3,2,1,0:T(8,128)S(1)} %slice.152), channel_id=1, source_target_pairs={{0,2},{1,3},{2,0},{3,1},{4,6},{5,7},{6,4},{7,5},{8,10},{9,11},{10,... | collective-permute-start | bytes 393224 | tf_op jit(solution)/shard_map/ppermute | solution.py:601
  81.1 0.0 collective-permute-done.18.refs_3_
  81.1 0.0 collective-permute-done.20.refs_5_
  81.1 0.0 collective-permute-done.19.refs_4_
  81.1 1.9 %put_in_place.2.refs_4_ = f32[8,32,8,256]{3,2,1,0:T(8,128)} custom-call(s32[1,3]{1,0:T(1,128)S(1)} %add_bitcast_fusion.here_ref, f32[4,8,8,256]{3,2,1,0:T(8,128)S(1)} %pad_maximum_fusion.refs_0_, f32[4,8,8,256]{3,2,1,0:T(8,128)S(1)} %collective-permute-done.14.refs_1_, f32[4,8,8,256]{3,2,1,0:T(8,128)S(1)} %collective-permute-done.16.refs_2_, ...), custom_call_target="tpu_custom_call" | custom-call | bytes 4194304 | tf_op jit(solution)/shard_map/put_in_place/pallas_call | solution.py:565
  83.0 2.1 %collective-permute-done.17.refs_1_ = f32[2,8,8,256]{3,2,1,0:T(8,128)S(1)} collective-permute-done((f32[2,8,8,256]{3,2,1,0:T(8,128)S(1)}, f32[2,8,8,256]{3,2,1,0:T(8,128)S(1)}, u32[]{:S(2)}, u32[]{:S(2)}) %collective-permute-start.17) | collective-permute-done | bytes 131104 | tf_op jit(solution)/shard_map/ppermute | solution.py:601
  85.1 0.4 collective-permute-done.15.refs_0_
  85.6 0.0 collective-permute-start.21
  85.6 0.5 collective-permute-start.22
  86.1 0.8 collective-permute-done.21.refs_2_
  86.9 0.2 collective-permute-done.22.refs_3_
  87.1 1.4 %put_in_place.3 = f32[8,32,8,256]{3,2,1,0:T(8,128)} custom-call(s32[1,3]{1,0:T(1,128)S(1)} %add_bitcast_fusion.here_ref, f32[2,8,8,256]{3,2,1,0:T(8,128)S(1)} %collective-permute-done.15.refs_0_, f32[2,8,8,256]{3,2,1,0:T(8,128)S(1)} %collective-permute-done.17.refs_1_, ...), custom_call_target="tpu_custom_call", output_to_operand_aliasing={{}: (5, {})} | custom-call | bytes 4194304 | tf_op jit(solution)/shard_map/put_in_place/pallas_call | solution.py:565
  (15 shorter events, 0.2 us)
Async XLA Ops:
  0.6 3.8 %copy-start.5 = (s32[4,2]{0,1:T(2,128)S(1)}, s32[4,2]{0,1:T(2,128)}, u32[]{:S(2)}) copy-start(s32[4,2]{0,1:T(2,128)} %param.13) | copy-start | bytes 100
  0.6 1.6 %copy-start = (f32[512,2,512]{2,1,0:T(2,128)S(1)}, f32[512,2,512]{2,1,0:T(2,128)}, u32[]{:S(2)}) copy-start(f32[512,2,512]{2,1,0:T(2,128)} %param.10) | copy-start | bytes 6291460
  2.2 2.5 %copy-start.1 = (f32[512,2,512]{2,1,0:T(2,128)S(1)}, f32[512,2,512]{2,1,0:T(2,128)}, u32[]{:S(2)}) copy-start(f32[512,2,512]{2,1,0:T(2,128)} %param.10) | copy-start | bytes 6291460
  2.3 19.1 %collective-permute-start = (f32[2048,128]{1,0:T(8,128)S(1)}, f32[2048,128]{1,0:T(8,128)}, u32[]{:S(2)}, u32[]{:S(2)}) collective-permute-start(f32[2048,128]{1,0:T(8,128)S(1)} %first_rows.1), channel_id=1, source_target_pairs={{4,0},{8,4},{12,8},{16,12},{20,16},{24,20},{28,24},{5,1},{9,5},{13... | collective-permute-start | bytes 3145736 | tf_op jit(solution)/shard_map/ppermute | solution.py:22
  4.7 1.6 %copy-start.2 = (f32[4,2,256,256]{3,2,1,0:T(8,128)S(1)}, f32[4,2,256,256]{3,2,1,0:T(8,128)}, u32[]{:S(2)}) copy-start(f32[4,2,256,256]{3,2,1,0:T(8,128)} %probe_ref.1) | copy-start | bytes 6291460
  6.3 1.2 %copy-start.3 = (f32[4,256,256]{2,1,0:T(8,128)S(1)}, f32[4,256,256]{2,1,0:T(8,128)}, u32[]{:S(2)}) copy-start(f32[4,256,256]{2,1,0:T(8,128)} %diffraction_ref.1) | copy-start | bytes 3145732
  7.5 1.0 %copy-start.4 = (f32[8,128,128]{2,1,0:T(8,128)S(1)}, f32[8,128,128]{2,1,0:T(8,128)}, u32[]{:S(2)}) copy-start(f32[8,128,128]{2,1,0:T(8,128)} %constant.93.clone.factor_ref) | copy-start | bytes 1572868
  32.9 1.6 %collective-permute-start.1 = (f32[4,9,8,256]{3,2,1,0:T(8,128)S(1)}, f32[4,9,8,256]{3,2,1,0:T(8,128)S(1)}, u32[]{:S(2)}, u32[]{:S(2)}) collective-permute-start(f32[4,9,8,256]{3,2,1,0:T(8,128)S(1)} %get-tuple-element.73), channel_id=1, source_target_pairs={{0,4},{4,0},{8,12},{12,8},{16,20},{20,16},{24,28},{28,24},{1,5},{5... | collective-permute-start | bytes 884744 | tf_op jit(solution)/shard_map/ppermute | solution.py:605
  34.6 4.3 %collective-permute-start.2 = (f32[3,4,9,8,256]{4,3,2,1,0:T(8,128)S(1)}, f32[3,4,9,8,256]{4,3,2,1,0:T(8,128)S(1)}, u32[]{:S(2)}, u32[]{:S(2)}) collective-permute-start(f32[3,4,9,8,256]{4,3,2,1,0:T(8,128)S(1)} %get-tuple-element.74), channel_id=1, source_target_pairs={{0,4},{4,0},{8,12},{12,8},{16,20},{20,16},{24,28},{28,24},{1,5},{5... | collective-permute-start | bytes 2654216 | tf_op jit(solution)/shard_map/ppermute | solution.py:605
  34.8 6.3 %collective-permute-start.5 = (f32[2,9,8,256]{3,2,1,0:T(8,128)S(1)}, f32[2,9,8,256]{3,2,1,0:T(8,128)S(1)}, u32[]{:S(2)}, u32[]{:S(2)}) collective-permute-start(f32[2,9,8,256]{3,2,1,0:T(8,128)S(1)} %get-tuple-element.106), channel_id=1, source_target_pairs={{0,1},{1,0},{2,3},{3,2},{4,5},{5,4},{6,7},{7,6},{8,9},{9,8},{10,11... | collective-permute-start | bytes 442376 | tf_op jit(solution)/shard_map/ppermute | solution.py:601
  34.8 8.2 %collective-permute-start.3 = (f32[2,9,8,256]{3,2,1,0:T(8,128)S(1)}, f32[2,9,8,256]{3,2,1,0:T(8,128)S(1)}, u32[]{:S(2)}, u32[]{:S(2)}) collective-permute-start(f32[2,9,8,256]{3,2,1,0:T(8,128)S(1)} %get-tuple-element.107), channel_id=1, source_target_pairs={{0,2},{1,3},{2,0},{3,1},{4,6},{5,7},{6,4},{7,5},{8,10},{9,11},{10,... | collective-permute-start | bytes 442376 | tf_op jit(solution)/shard_map/ppermute | solution.py:601
  39.0 24.5 %collective-permute-start.10 = (f32[2048,128]{1,0:T(8,128)S(1)}, f32[2048,128]{1,0:T(8,128)S(1)}, u32[]{:S(2)}, u32[]{:S(2)}) collective-permute-start(f32[2048,128]{1,0:T(8,128)S(1)} %get-tuple-element.84), channel_id=1, source_target_pairs={{0,4},{4,8},{8,12},{12,16},{16,20},{20,24},{24,28},{1,5},{5,9},{9,... | collective-permute-start | bytes 3145736 | tf_op jit(solution)/shard_map/ppermute | solution.py:22
  43.1 9.7 %collective-permute-start.6 = (f32[4,9,8,256]{3,2,1,0:T(8,128)S(1)}, f32[4,9,8,256]{3,2,1,0:T(8,128)S(1)}, u32[]{:S(2)}, u32[]{:S(2)}) collective-permute-start(f32[4,9,8,256]{3,2,1,0:T(8,128)S(1)} %get-tuple-element.102), channel_id=1, source_target_pairs={{0,2},{1,3},{2,0},{3,1},{4,6},{5,7},{6,4},{7,5},{8,10},{9,11},{10,... | collective-permute-start | bytes 884744 | tf_op jit(solution)/shard_map/ppermute | solution.py:601
  44.9 8.5 %collective-permute-start.4 = (f32[4,9,8,256]{3,2,1,0:T(8,128)S(1)}, f32[4,9,8,256]{3,2,1,0:T(8,128)S(1)}, u32[]{:S(2)}, u32[]{:S(2)}) collective-permute-start(f32[4,9,8,256]{3,2,1,0:T(8,128)S(1)} %get-tuple-element.103), channel_id=1, source_target_pairs={{0,1},{1,0},{2,3},{3,2},{4,5},{5,4},{6,7},{7,6},{8,9},{9,8},{10,11... | collective-permute-start | bytes 884744 | tf_op jit(solution)/shard_map/ppermute | solution.py:601
  53.4 5.3 %collective-permute-start.9 = (f32[9,8,256]{2,1,0:T(8,128)S(1)}, f32[9,8,256]{2,1,0:T(8,128)S(1)}, u32[]{:S(2)}, u32[]{:S(2)}) collective-permute-start(f32[9,8,256]{2,1,0:T(8,128)S(1)} %get-tuple-element.98), channel_id=1, source_target_pairs={{0,24},{4,28},{8,0},{12,4},{16,8},{20,12},{24,16},{28,20},{1,25},{... | collective-permute-start | bytes 221192 | tf_op jit(solution)/shard_map/ppermute | solution.py:610
  56.7 6.7 %collective-permute-start.8 = (f32[9,8,256]{2,1,0:T(8,128)S(1)}, f32[9,8,256]{2,1,0:T(8,128)S(1)}, u32[]{:S(2)}, u32[]{:S(2)}) collective-permute-start(f32[9,8,256]{2,1,0:T(8,128)S(1)} %get-tuple-element.99), channel_id=1, source_target_pairs={{0,16},{4,20},{8,24},{12,28},{16,0},{20,4},{24,8},{28,12},{1,17},{... | collective-permute-start | bytes 221192 | tf_op jit(solution)/shard_map/ppermute | solution.py:610
  56.8 6.7 %collective-permute-start.7 = (f32[9,8,256]{2,1,0:T(8,128)S(1)}, f32[9,8,256]{2,1,0:T(8,128)S(1)}, u32[]{:S(2)}, u32[]{:S(2)}) collective-permute-start(f32[9,8,256]{2,1,0:T(8,128)S(1)} %get-tuple-element.100), channel_id=1, source_target_pairs={{0,8},{4,12},{8,16},{12,20},{16,24},{20,28},{24,0},{28,4},{1,9},{5... | collective-permute-start | bytes 221192 | tf_op jit(solution)/shard_map/ppermute | solution.py:610
  63.5 4.3 %collective-permute-start.13 = (f32[8,8,256]{2,1,0:T(8,128)S(1)}, f32[8,8,256]{2,1,0:T(8,128)S(1)}, u32[]{:S(2)}, u32[]{:S(2)}) collective-permute-start(f32[8,8,256]{2,1,0:T(8,128)S(1)} %divided.1), channel_id=1, source_target_pairs={{0,24},{4,28},{8,0},{12,4},{16,8},{20,12},{24,16},{28,20},{1,25},{... | collective-permute-start | bytes 196616 | tf_op jit(solution)/shard_map/ppermute | solution.py:610
  64.7 6.6 %collective-permute-start.12 = (f32[8,8,256]{2,1,0:T(8,128)S(1)}, f32[8,8,256]{2,1,0:T(8,128)S(1)}, u32[]{:S(2)}, u32[]{:S(2)}) collective-permute-start(f32[8,8,256]{2,1,0:T(8,128)S(1)} %divided.1), channel_id=1, source_target_pairs={{0,16},{4,20},{8,24},{12,28},{16,0},{20,4},{24,8},{28,12},{1,17},{... | collective-permute-start | bytes 196616 | tf_op jit(solution)/shard_map/ppermute | solution.py:610
  64.7 6.6 %collective-permute-start.11 = (f32[8,8,256]{2,1,0:T(8,128)S(1)}, f32[8,8,256]{2,1,0:T(8,128)S(1)}, u32[]{:S(2)}, u32[]{:S(2)}) collective-permute-start(f32[8,8,256]{2,1,0:T(8,128)S(1)} %divided.1), channel_id=1, source_target_pairs={{0,8},{4,12},{8,16},{12,20},{16,24},{20,28},{24,0},{28,4},{1,9},{5... | collective-permute-start | bytes 196616 | tf_op jit(solution)/shard_map/ppermute | solution.py:610
  71.3 6.4 %collective-permute-start.16 = (f32[4,8,8,256]{3,2,1,0:T(8,128)S(1)}, f32[4,8,8,256]{3,2,1,0:T(8,128)S(1)}, u32[]{:S(2)}, u32[]{:S(2)}) collective-permute-start(f32[4,8,8,256]{3,2,1,0:T(8,128)S(1)} %pad_maximum_fusion.refs_0_), channel_id=1, source_target_pairs={{0,2},{1,3},{2,0},{3,1},{4,6},{5,7},{6,4},{7,5},{8,10},{9,11},{10,... | collective-permute-start | bytes 786440 | tf_op jit(solution)/shard_map/ppermute | solution.py:601
  72.8 6.4 %collective-permute-start.14 = (f32[4,8,8,256]{3,2,1,0:T(8,128)S(1)}, f32[4,8,8,256]{3,2,1,0:T(8,128)S(1)}, u32[]{:S(2)}, u32[]{:S(2)}) collective-permute-start(f32[4,8,8,256]{3,2,1,0:T(8,128)S(1)} %pad_maximum_fusion.refs_0_), channel_id=1, source_target_pairs={{0,1},{1,0},{2,3},{3,2},{4,5},{5,4},{6,7},{7,6},{8,9},{9,8},{10,11... | collective-permute-start | bytes 786440 | tf_op jit(solution)/shard_map/ppermute | solution.py:601
  73.4 7.7 %collective-permute-start.18 = (f32[4,8,8,256]{3,2,1,0:T(8,128)S(1)}, f32[4,8,8,256]{3,2,1,0:T(8,128)S(1)}, u32[]{:S(2)}, u32[]{:S(2)}) collective-permute-start(f32[4,8,8,256]{3,2,1,0:T(8,128)S(1)} %pad_maximum_fusion.refs_0_), channel_id=1, source_target_pairs={{0,4},{4,0},{8,12},{12,8},{16,20},{20,16},{24,28},{28,24},{1,5},{5... | collective-permute-start | bytes 786440 | tf_op jit(solution)/shard_map/ppermute | solution.py:605
  77.8 3.3 %collective-permute-start.20 = (f32[4,8,8,256]{3,2,1,0:T(8,128)S(1)}, f32[4,8,8,256]{3,2,1,0:T(8,128)S(1)}, u32[]{:S(2)}, u32[]{:S(2)}) collective-permute-start(f32[4,8,8,256]{3,2,1,0:T(8,128)S(1)} %collective-permute-done.16.refs_2_), channel_id=1, source_target_pairs={{0,4},{4,0},{8,12},{12,8},{16,20},{20,16},{24,28},{28,24},{1,5},{5... | collective-permute-start | bytes 786440 | tf_op jit(solution)/shard_map/ppermute | solution.py:605
  79.1 2.0 %collective-permute-start.19 = (f32[4,8,8,256]{3,2,1,0:T(8,128)S(1)}, f32[4,8,8,256]{3,2,1,0:T(8,128)S(1)}, u32[]{:S(2)}, u32[]{:S(2)}) collective-permute-start(f32[4,8,8,256]{3,2,1,0:T(8,128)S(1)} %collective-permute-done.14.refs_1_), channel_id=1, source_target_pairs={{0,4},{4,0},{8,12},{12,8},{16,20},{20,16},{24,28},{28,24},{1,5},{5... | collective-permute-start | bytes 786440 | tf_op jit(solution)/shard_map/ppermute | solution.py:605
  79.2 6.0 %collective-permute-start.17 = (f32[2,8,8,256]{3,2,1,0:T(8,128)S(1)}, f32[2,8,8,256]{3,2,1,0:T(8,128)S(1)}, u32[]{:S(2)}, u32[]{:S(2)}) collective-permute-start(f32[2,8,8,256]{3,2,1,0:T(8,128)S(1)} %slice.153), channel_id=1, source_target_pairs={{0,1},{1,0},{2,3},{3,2},{4,5},{5,4},{6,7},{7,6},{8,9},{9,8},{10,11... | collective-permute-start | bytes 393224 | tf_op jit(solution)/shard_map/ppermute | solution.py:601
  79.9 5.7 %collective-permute-start.15 = (f32[2,8,8,256]{3,2,1,0:T(8,128)S(1)}, f32[2,8,8,256]{3,2,1,0:T(8,128)S(1)}, u32[]{:S(2)}, u32[]{:S(2)}) collective-permute-start(f32[2,8,8,256]{3,2,1,0:T(8,128)S(1)} %slice.152), channel_id=1, source_target_pairs={{0,2},{1,3},{2,0},{3,1},{4,6},{5,7},{6,4},{7,5},{8,10},{9,11},{10,... | collective-permute-start | bytes 393224 | tf_op jit(solution)/shard_map/ppermute | solution.py:601
  85.6 1.3 %collective-permute-start.21 = (f32[2,8,8,256]{3,2,1,0:T(8,128)S(1)}, f32[2,8,8,256]{3,2,1,0:T(8,128)S(1)}, u32[]{:S(2)}, u32[]{:S(2)}) collective-permute-start(f32[2,8,8,256]{3,2,1,0:T(8,128)S(1)} %collective-permute-done.15.refs_0_), channel_id=1, source_target_pairs={{0,4},{4,0},{8,12},{12,8},{16,20},{20,16},{24,28},{28,24},{1,5},{5... | collective-permute-start | bytes 393224 | tf_op jit(solution)/shard_map/ppermute | solution.py:605
  85.6 1.5 %collective-permute-start.22 = (f32[2,8,8,256]{3,2,1,0:T(8,128)S(1)}, f32[2,8,8,256]{3,2,1,0:T(8,128)S(1)}, u32[]{:S(2)}, u32[]{:S(2)}) collective-permute-start(f32[2,8,8,256]{3,2,1,0:T(8,128)S(1)} %collective-permute-done.17.refs_1_), channel_id=1, source_target_pairs={{0,4},{4,0},{8,12},{12,8},{16,20},{20,16},{24,28},{28,24},{1,5},{5... | collective-permute-start | bytes 393224 | tf_op jit(solution)/shard_map/ppermute | solution.py:605
